TPU v7x, 512 devices: a whole 4x4x16 slice. The times are simulated.
512 devices in a mesh: ctx: 16 (over z_lo, x), sample: 32 (over z_hi, y, core).
Axes of the slice: x: 4, y: 4, z: 16 (z_hi: 4, z_lo: 4; z = z_hi * 4 + z_lo), core: 2. Of those that a mesh axis runs over, the one named last changes fastest.
Arguments:
- prompt_latent: bfloat16 [2, 4096, 576], P(None, ('ctx', 'sample')), may hold values from -8 to 8
- suffix_latent: bfloat16 [32, 256, 576], P('sample', 'ctx'), may hold values from -6 to 6
- queries: bfloat16 [32, 5, 128, 192], P(None, None, 'sample'), may hold values from -700 to 700
- key_up: bfloat16 [128, 128, 512], P('sample'), may hold values from -0.5 to 0.5
- value_up: bfloat16 [128, 512, 128], P('sample'), may hold values from -0.25 to 0.25
- out_grad: bfloat16 [32, 5, 128, 128], P(None, None, 'sample'), may hold values from -6 to 6
- fork_prompt: int32 [32], replicated, may hold values from 0 to 1, as said below
- suffix_length: int32 [32], replicated, may hold values from 5 to 256, as said below
Outputs:
- prompt_grad: float32 [2, 4096, 576], P(None, ('ctx', 'sample'))
- suffix_grad: float32 [32, 256, 576], P('sample', 'ctx')
- query_grad: float32 [32, 5, 128, 192], P(None, None, 'sample')
- key_up_grad: float32 [128, 128, 512], P('sample')
- value_up_grad: float32 [128, 512, 128], P('sample')
Inputs may be any that keep to these rules, and one draw needn't show every extreme that they name: `fork_prompt`: each prompt has exactly 16 forks. `suffix_length`: the largest suffix length is 256 in every draw.
All inputs are finite; a program needn't handle non-finite values.
Results may differ from a plain program's by a relative error of at most 0.03.
Values may be sent and summed in bfloat16 or wider, within the bound.
A program may use at most 128 MiB of HBM per device.

v0:
```python
import jax
import jax.numpy as jnp
from jax import lax
from jax.sharding import PartitionSpec as P

NEG_FILL = -1e30


def combined_all(x, axis, combine):
    everything = jax.tree.map(lambda part: lax.all_gather(part, axis), x)
    first = jax.tree.map(lambda part: part[0], everything)

    def step(k, so_far):
        return combine(so_far, jax.tree.map(lambda part: part[k], everything))

    return lax.fori_loop(1, lax.axis_size(axis), step, first)


def combine_rows(left_part, right_part):
    peak_val = jnp.maximum(left_part[0], right_part[0])
    left_weight = jnp.exp(left_part[0] - peak_val)
    right_weight = jnp.exp(right_part[0] - peak_val)
    return (
        peak_val,
        left_part[1] * left_weight + right_part[1] * right_weight,
        left_part[2] * left_weight[..., None] + right_part[2] * right_weight[..., None],
    )


def grads_of_keys(score_grad, query_rows, prob_half, lgrad_rows):
    latent_width = lgrad_rows.shape[-1]
    key_grad = jnp.einsum(
        "prk,prc->pkc", score_grad, query_rows, preferred_element_type=jnp.float32
    )
    value_grad = jnp.einsum(
        "prk,prl->pkl", prob_half, lgrad_rows, preferred_element_type=jnp.float32
    )
    return jnp.concatenate(
        [key_grad[..., :latent_width] + value_grad, key_grad[..., latent_width:]], -1
    )


def split_halves(weights):
    upper = weights.astype(jnp.bfloat16)
    lower = (weights - upper.astype(jnp.float32)).astype(jnp.bfloat16)
    return (upper, lower)


def shards(
    prompt_latent, suffix_latent, queries, key_up, value_up, out_grad, fork_prompt, suffix_length
):
    fork_count, recomp_count, head_local, query_width = queries.shape
    nope_width = key_up.shape[1]
    latent_width = key_up.shape[2]
    prompt_count = prompt_latent.shape[0]
    group_forks = fork_count // prompt_count
    row_count = recomp_count * head_local
    score_scale = query_width ** (-0.5)
    highest = lax.Precision.HIGHEST
    prompt_keys, suffix_keys = (
        lax.all_gather(prompt_latent, "sample", axis=1, tiled=True),
        lax.all_gather(suffix_latent, "sample", axis=0, tiled=True),
    )
    block_len = prompt_keys.shape[1]
    suffix_len = suffix_keys.shape[1]
    full_width = prompt_keys.shape[2]
    fork_order = jnp.argsort(fork_prompt, stable=True)
    inverse = jnp.argsort(fork_order)
    query_lat = jnp.einsum(
        "frhn,hnl->frhl", queries[..., :nope_width], key_up, preferred_element_type=jnp.float32
    ).astype(jnp.bfloat16)
    absorbed = jnp.concatenate([query_lat, queries[..., nope_width:]], -1)[fork_order].reshape(
        fork_count, row_count, full_width
    )
    latent_grad = jnp.einsum(
        "frhv,hlv->frhl", out_grad, value_up, preferred_element_type=jnp.float32
    ).astype(jnp.bfloat16)
    latent_grad = latent_grad[fork_order].reshape(fork_count, row_count, latent_width)
    grouped_query = absorbed.reshape(prompt_count, group_forks * row_count, full_width)
    grouped_lgrad = latent_grad.reshape(prompt_count, group_forks * row_count, latent_width)
    prompt_scores = (
        jnp.einsum("prc,pkc->prk", grouped_query, prompt_keys, preferred_element_type=jnp.float32)
        * score_scale
    )
    prompt_scores = prompt_scores.reshape(fork_count, row_count, block_len)
    sorted_suffix = suffix_keys[fork_order]
    sorted_length = suffix_length[fork_order]
    suffix_scores = (
        jnp.einsum("frc,fkc->frk", absorbed, sorted_suffix, preferred_element_type=jnp.float32)
        * score_scale
    )
    position = lax.axis_index("ctx") * suffix_len + jnp.arange(suffix_len, dtype=jnp.int32)
    row_step = jnp.arange(row_count, dtype=jnp.int32) // head_local
    visible = (
        position[None, None, :]
        <= sorted_length[:, None, None] - recomp_count + row_step[None, :, None]
    )
    suffix_scores = jnp.where(visible, suffix_scores, NEG_FILL)
    local_peak = jnp.maximum(jnp.max(prompt_scores, -1), jnp.max(suffix_scores, -1))
    prompt_values = prompt_keys[..., :latent_width]
    suffix_values = sorted_suffix[..., :latent_width]
    prompt_exp = jnp.exp(prompt_scores - local_peak[..., None])
    suffix_exp = jnp.where(visible, jnp.exp(suffix_scores - local_peak[..., None]), 0.0)
    local_total = jnp.sum(prompt_exp, -1) + jnp.sum(suffix_exp, -1)
    grouped = prompt_exp.reshape(prompt_count, group_forks * row_count, block_len)
    prompt_upper, prompt_lower = split_halves(grouped)
    prompt_side = jnp.einsum(
        "prk,pkl->prl", prompt_upper, prompt_values, preferred_element_type=jnp.float32
    )
    prompt_side = prompt_side + jnp.einsum(
        "prk,pkl->prl", prompt_lower, prompt_values, preferred_element_type=jnp.float32
    )
    prompt_side = prompt_side.reshape(fork_count, row_count, latent_width)
    suffix_upper, suffix_lower = split_halves(suffix_exp)
    suffix_side = jnp.einsum(
        "frk,fkl->frl", suffix_upper, suffix_values, preferred_element_type=jnp.float32
    )
    suffix_side = suffix_side + jnp.einsum(
        "frk,fkl->frl", suffix_lower, suffix_values, preferred_element_type=jnp.float32
    )
    local_acc = prompt_side + suffix_side
    row_peak, row_total, row_acc = combined_all(
        (local_peak, local_total, local_acc), "ctx", combine_rows
    )
    latent_out = row_acc / row_total[..., None]
    log_sum = row_peak + jnp.log(row_total)
    prompt_prob = jnp.exp(prompt_scores - log_sum[..., None])
    suffix_prob = jnp.where(visible, jnp.exp(suffix_scores - log_sum[..., None]), 0.0)
    prompt_pgrad = jnp.einsum(
        "prl,pkl->prk", grouped_lgrad, prompt_values, preferred_element_type=jnp.float32
    )
    prompt_pgrad = prompt_pgrad.reshape(fork_count, row_count, block_len)
    suffix_pgrad = jnp.einsum(
        "frl,fkl->frk", latent_grad, suffix_values, preferred_element_type=jnp.float32
    )
    sorted_out = out_grad[fork_order].astype(jnp.float32)
    row_delta = jnp.sum(latent_grad.astype(jnp.float32) * latent_out, -1)
    value_up_grad = jnp.einsum(
        "frhl,frhv->hlv",
        latent_out.reshape(fork_count, recomp_count, head_local, latent_width),
        sorted_out,
        precision=highest,
    )
    prompt_sgrad = (prompt_prob * (prompt_pgrad - row_delta[..., None]) * score_scale).astype(
        jnp.bfloat16
    )
    suffix_sgrad = (suffix_prob * (suffix_pgrad - row_delta[..., None]) * score_scale).astype(
        jnp.bfloat16
    )
    grouped_sgrad = prompt_sgrad.reshape(prompt_count, group_forks * row_count, block_len)
    grouped_prob = prompt_prob.astype(jnp.bfloat16).reshape(
        prompt_count, group_forks * row_count, block_len
    )
    local_qgrad = jnp.einsum(
        "prk,pkc->prc", grouped_sgrad, prompt_keys, preferred_element_type=jnp.float32
    )
    local_qgrad = local_qgrad.reshape(fork_count, row_count, full_width)
    local_qgrad = local_qgrad + jnp.einsum(
        "frk,fkc->frc", suffix_sgrad, sorted_suffix, preferred_element_type=jnp.float32
    )
    suffix_part = grads_of_keys(
        suffix_sgrad, absorbed, suffix_prob.astype(jnp.bfloat16), latent_grad
    )[inverse]
    prompt_part = grads_of_keys(grouped_sgrad, grouped_query, grouped_prob, grouped_lgrad)
    prompt_grad, suffix_grad = (
        lax.psum_scatter(
            prompt_part.astype(jnp.bfloat16), "sample", scatter_dimension=1, tiled=True
        ).astype(jnp.float32),
        lax.psum_scatter(
            suffix_part.astype(jnp.bfloat16), "sample", scatter_dimension=0, tiled=True
        ).astype(jnp.float32),
    )
    fork_qgrad = local_qgrad[inverse].reshape(fork_count, recomp_count, head_local, full_width)
    query_nope = queries[..., :nope_width].astype(jnp.float32)
    key_up32 = key_up.astype(jnp.float32)
    summed_qgrad = lax.psum(fork_qgrad.astype(jnp.bfloat16), "ctx").astype(jnp.float32)
    grad_nope = jnp.einsum(
        "frhl,hnl->frhn", summed_qgrad[..., :latent_width], key_up32, precision=highest
    )
    query_part = jnp.concatenate([grad_nope, summed_qgrad[..., latent_width:]], -1)
    weight_part = jnp.einsum(
        "frhn,frhl->hnl", query_nope, summed_qgrad[..., :latent_width], precision=highest
    )
    return (prompt_grad, suffix_grad, query_part, weight_part, value_up_grad)


def solution(mesh):
    return jax.shard_map(
        shards,
        mesh=mesh,
        in_specs=(
            P(None, ("ctx", "sample"), None),
            P("sample", "ctx", None),
            P(None, None, "sample", None),
            P("sample", None, None),
            P("sample", None, None),
            P(None, None, "sample", None),
            P(),
            P(),
        ),
        out_specs=(
            P(None, ("ctx", "sample"), None),
            P("sample", "ctx", None),
            P(None, None, "sample", None),
            P("sample", None, None),
            P("sample", None, None),
        ),
        check_vma=False,
    )
```

profile of v0, /device:TPU:6, one launch (start us, length us, event | category | flops | bytes accessed | tf_op | source)
XLA Modules:
  0.0 1075.0 jit_solution(1181817301098696718)
XLA Ops:
  9.3 2.3 sort.34
  16.0 64.0 %all_gather.21 = bf16[32,16,576]{2,1,0:T(8,128)(2,1)} all-gather(bf16[1,16,576]{2,1,0:T(8,128)(2,1)S(1)} %copy-done.26), channel_id=1, replica_groups=mesh['ctx'=16,'sample'=32] {'sample'}, dimensions={0}, use_global_device_ids=true | all-gather | bytes 608256 | tf_op jit(solution)/shard_map/all_gather | solution.py:62
  80.0 1.8 gather_fusion.2
  83.2 50.6 %all_gather.20 = bf16[2,256,576]{2,1,0:T(8,128)(2,1)S(1)} all-gather(bf16[2,8,576]{2,1,0:T(8,128)(2,1)S(1)} %copy-done.27), channel_id=1, replica_groups=mesh['ctx'=16,'sample'=32] {'sample'}, dimensions={1}, use_global_device_ids=true | all-gather | bytes 608256 | tf_op jit(solution)/shard_map/all_gather | solution.py:61
  134.8 1.5 convolution_add_fusion.1
  136.3 2.5 reshape.141
  140.8 1.9 copy.126
  148.4 1.6 sort.35
  150.0 35.9 %all_gather.23 = f32[16,32,20]{1,2,0:T(8,128)S(1)} all-gather(f32[1,32,20]{1,2,0:T(8,128)S(1)} %copy.125), channel_id=1, replica_groups=mesh['ctx'=16,'sample'=32] {'ctx'}, dimensions={0}, use_global_device_ids=true | all-gather | bytes 43520 | tf_op jit(solution)/shard_map/all_gather | solution.py:10
  186.0 41.3 %all_gather.22 = f32[16,32,20]{1,2,0:T(8,128)S(1)} all-gather(f32[1,32,20]{1,2,0:T(8,128)S(1)} %copy.124), channel_id=1, replica_groups=mesh['ctx'=16,'sample'=32] {'ctx'}, dimensions={0}, use_global_device_ids=true | all-gather | bytes 43520 | tf_op jit(solution)/shard_map/all_gather | solution.py:10
  227.9 141.3 %all-gather.3.cloned.1.call-done = f32[512,20,512]{2,0,1:T(8,128)} async-done(((f32[32,20,512]{2,0,1:T(8,128)}), f32[512,20,512]{2,0,1:T(8,128)}) %all-gather.3.cloned.1.call-update) | async-done | bytes 20971536 | tf_op jit(solution)/shard_map/all_gather | solution.py:10
  371.3 55.4 %while.19 = (s32[]{:T(128)}, f32[32,20]{0,1:T(8,128)S(1)}, f32[32,20]{0,1:T(8,128)S(1)}, f32[32,20,512]{2,1,0:T(8,128)S(1)}, f32[16,32,20]{1,2,0:T(8,128)}, /*in...) while((s32[]{:T(128)}, f32[32,20]{0,1:T(8,128)S(1)}, ...), condition=%wide.region_6.7_spmd, body=%wide.region_5.6_spmd.sunk | while | flops 986885 | bytes 6589591 | solution.py:16
  372.2 1.4 constant_dynamic-slice_fusion.2
  373.7 1.3 fusion.85
  375.9 1.4 constant_dynamic-slice_fusion.2
  379.6 1.4 constant_dynamic-slice_fusion.2
  383.3 1.4 constant_dynamic-slice_fusion.2
  387.0 1.4 constant_dynamic-slice_fusion.2
  388.4 1.3 fusion.85
  390.7 1.4 constant_dynamic-slice_fusion.2
  392.1 1.3 fusion.85
  394.4 1.4 constant_dynamic-slice_fusion.2
  398.1 1.4 constant_dynamic-slice_fusion.2
  401.8 1.4 constant_dynamic-slice_fusion.2
  405.5 1.4 constant_dynamic-slice_fusion.2
  406.9 1.3 fusion.85
  409.2 1.4 constant_dynamic-slice_fusion.2
  410.6 1.3 fusion.85
  412.9 1.4 constant_dynamic-slice_fusion.2
  416.6 1.4 constant_dynamic-slice_fusion.2
  420.3 1.4 constant_dynamic-slice_fusion.2
  424.0 1.4 constant_dynamic-slice_fusion.2
  427.0 3.0 multiply_reduce_fusion
  430.7 1.5 fusion.9
  434.0 1.8 copy.136
  435.8 1.6 fusion.68
  437.4 1.5 reshape.143
  439.1 1.6 fusion.13
  440.7 1.5 convolution_add_fusion
  442.2 2.1 gather_fusion.5
  445.5 1.5 gather_fusion.6
  450.8 1.7 gather_fusion.4
  452.6 2.8 convolution_bitcast_fusion.1
  455.4 323.3 %all-reduce.6.cloned.1.call-done = bf16[2,256,576]{2,0,1:T(2,128)(2,1)} async-done(((bf16[2,256,576]{2,0,1:T(2,128)(2,1)}), bf16[2,256,576]{2,0,1:T(2,128)(2,1)}) %all-reduce.6.cloned.1.call-update) | async-done | bytes 589840
  780.0 168.1 %all-reduce.4.cloned.1.call-done = bf16[32,5,4,576]{3,0,1,2:T(8,128)(2,1)} async-done(((bf16[32,5,4,576]{3,0,1,2:T(8,128)(2,1)}), bf16[32,5,4,576]{3,0,1,2:T(8,128)(2,1)}) %all-reduce.4.cloned.1.call-update) | async-done | bytes 737296 | tf_op jit(solution)/shard_map/psum | solution.py:176
  948.1 1.6 convolution_bitcast_fusion
  952.7 114.4 %reduce-scatter.2.cloned.1.call-done = bf16[1,16,576]{2,1,0:T(8,128)(2,1)} async-done(((bf16[32,16,576]{2,1,0:T(8,128)(2,1)}), bf16[1,16,576]{2,1,0:T(8,128)(2,1)}) %reduce-scatter.2.cloned.1.call-update) | async-done | bytes 18448 | tf_op jit(solution)/shard_map/reduce_scatter | solution.py:169
  1067.1 1.3 convert_element_type.84
  (201 shorter events, 57.9 us)
Async XLA Ops:
  7.2 4.5 copy-start
  7.2 362.0 %all-gather.3.cloned.1.call-start = ((), (), s32[]{:S(2)}) async-start(), calls=%async_computation.3 | async-start | bytes 22282240 | tf_op jit(solution)/shard_map/all_gather | solution.py:10
  8.3 3.8 copy-start.18
  11.6 0.5 copy-start.32
  11.6 133.0 %copy-start.28 = (s32[1024]{0:T(1024)}, s32[1024]{0:T(1024)S(1)}, u32[]{:S(2)}) copy-start(s32[1024]{0:T(1024)S(1)} %pad_clamp_fusion.1) | copy-start | bytes 12292
  13.9 1.4 copy-start.1
  14.9 1.2 copy-start.26
  15.3 118.4 %copy-start.4 = (bf16[2,320,576]{2,1,0:T(8,128)(2,1)}, bf16[2,320,576]{2,1,0:T(8,128)(2,1)S(1)}, u32[]{:S(2)}) copy-start(bf16[2,320,576]{2,1,0:T(8,128)(2,1)S(1)} %reshape_reshape.6) | copy-start | bytes 2211844
  15.3 66.6 %copy-start.11 = (bf16[32,5,4,576]{3,0,2,1:T(8,128)(2,1)S(1)}, bf16[32,5,4,576]{3,0,2,1:T(8,128)(2,1)}, u32[]{:S(2)}) copy-start(bf16[32,5,4,576]{3,0,2,1:T(8,128)(2,1)} %copy.122) | copy-start | bytes 2211844
  81.8 57.6 %copy-start.2 = (bf16[32,16,576]{2,1,0:T(8,128)(2,1)}, bf16[32,16,576]{2,1,0:T(8,128)(2,1)S(1)}, u32[]{:S(2)}) copy-start(bf16[32,16,576]{2,1,0:T(8,128)(2,1)S(1)} %gather_fusion.2) | copy-start | bytes 1769476
  81.8 1.4 copy-start.27
  81.8 57.6 %copy-start.29 = (s32[16]{0:T(128)}, s32[16]{0:T(128)S(1)}, u32[]{:S(2)}) copy-start(s32[16]{0:T(128)S(1)} %iota_add_fusion) | copy-start | bytes 196
  136.3 2.5 copy-start.9
  138.8 1.4 copy-start.7
  142.6 0.9 copy-start.16
  142.6 1.1 copy-start.20
  142.7 636.0 %all-reduce.6.cloned.1.call-start = ((), (), s32[]{:S(2)}) async-start(), calls=%async_computation.4 | async-start | bytes 1310720
  146.7 1.4 copy-start.30
  146.7 1.7 copy-start.33
  186.0 183.2 %copy-start.21 = (f32[16,32,20]{1,2,0:T(8,128)}, f32[16,32,20]{1,2,0:T(8,128)S(1)}, u32[]{:S(2)}) copy-start(f32[16,32,20]{1,2,0:T(8,128)S(1)} %all_gather.23) | copy-start | bytes 122884
  227.2 142.0 %copy-start.22 = (f32[16,32,20]{1,2,0:T(8,128)}, f32[16,32,20]{1,2,0:T(8,128)S(1)}, u32[]{:S(2)}) copy-start(f32[16,32,20]{1,2,0:T(8,128)S(1)} %all_gather.22) | copy-start | bytes 122884
  369.2 1.3 slice-start
  426.9 3.1 copy-start.23
  429.9 2.3 copy-start.5
  430.0 0.6 copy-start.25
  432.2 1.1 copy-start.13
  435.8 512.3 %all-reduce.4.cloned.1.call-start = ((), (), s32[]{:S(2)}) async-start(), calls=%async_computation.2 | async-start | bytes 1638400 | tf_op jit(solution)/shard_map/psum | solution.py:176
  437.4 1.6 copy-start.3
  437.4 1.6 copy-start.10
  444.4 1.1 copy-start.17
  444.4 4.5 copy-start.12
  445.4 621.7 %reduce-scatter.2.cloned.1.call-start = ((), (), s32[]{:S(2)}) async-start(), calls=%async_computation.1 | async-start | bytes 675840 | tf_op jit(solution)/shard_map/reduce_scatter | solution.py:169
  448.9 1.1 copy-start.6
  448.9 1.1 copy-start.24
  448.9 1.1 copy-start.31
  450.8 1.8 copy-start.8
  450.8 1.8 copy-start.15
  452.6 495.5 %copy-start.19 = (bf16[32,5,4,128]{3,2,1,0:T(4,128)(2,1)S(1)}, bf16[32,5,4,128]{3,2,1,0:T(4,128)(2,1)}, u32[]{:S(2)}) copy-start(bf16[32,5,4,128]{3,2,1,0:T(4,128)(2,1)} %copy-done.18) | copy-start | bytes 491524
  949.7 1.3 copy-start.14
Sparse Core Ops, SparseCore 0:
  142.8 226.3 all-gather.2
  435.9 342.7 all-reduce.5
  781.9 166.1 all-reduce.3
  952.4 114.6 reduce-scatter.1
where the time goes:
time: 1080 us; the launch traced here: 1070 us
  waiting for transfers between devices  747 us (69%)
  blocking collectives  192 us (18%)
  local copies, waits for them, and re-layouts  60.1 us (6%)
  other arithmetic  41.7 us (4%)
  matrix products  18.7 us (2%)
  between operations  15 us (1%)
    unnamed x5, waiting for transfers between devices  323 us
    psum x1, waiting for transfers between devices, shards(): lax.psum(fork_qgrad.astype(jnp.bfloat16), 'ctx').astype(jnp.float32)  168 us
    all_gather x1, waiting for transfers between devices, combined_all(): everything = jax.tree.map(lambda part: lax.all_gather(part, axis), x)  141 us
    reduce_scatter x1, waiting for transfers between devices, shards(): lax.psum_scatter(suffix_part.astype(jnp.bfloat16), 'sample', scatter_dime...  114 us
    all_gather x2, blocking collectives, combined_all(): everything = jax.tree.map(lambda part: lax.all_gather(part, axis), x)  77.2 us
    all_gather x1, blocking collectives, shards(): lax.all_gather(suffix_latent, 'sample', axis=0, tiled=True)  64 us
    all_gather x1, blocking collectives, shards(): lax.all_gather(prompt_latent, 'sample', axis=1, tiled=True)  50.6 us
  transfers between devices with their start and end apart: 4, of which 4 were waited for; matrix products, arithmetic and copies ran while one was open for 3% of the time, Pallas kernels for 0%

commit v1 on v0

v1 whole, which is shorter than its diff:
```python
import functools

import jax
import jax.numpy as jnp
from jax import lax
from jax.experimental import pallas as pl
from jax.experimental.pallas import tpu as pltpu
from jax.sharding import PartitionSpec as P

MESH = pl.DeviceIdType.MESH
F32 = jnp.float32
BF16 = jnp.bfloat16
HIDDEN = -1e30

ZL, X, ZH, Y, CORE = 4, 4, 4, 4, 2
FORKS, RECOMP, HEADS = 32, 5, 4
NOPE, ROPE, LATENT, VHEAD = 128, 64, 512, 128
WIDTH = LATENT + ROPE
QUERY = NOPE + ROPE
ROWS = FORKS * RECOMP * HEADS
TILE = 128
TILES = ROWS // TILE
PKEYS, SKEYS = 8, 16
BLOCK = 2 * PKEYS + SKEYS
KEYS = CORE * ZH * BLOCK
SCALE = QUERY**-0.5
W1 = HEADS * LATENT // 16
W2 = 192
GRAY = (0, 1, 3, 2)


def dot(a, b):
    return jnp.dot(a, b, preferred_element_type=F32)


def dot_nt(a, b):
    return lax.dot_general(a, b, (((1,), (1,)), ((), ())), preferred_element_type=F32)


class Sems:
    def __init__(self, send, recv):
        self.send, self.recv, self.used, self.started = send, recv, 0, []

    def copy(self, src, dst, device):
        k = self.used
        self.used += 1
        made = pltpu.make_async_remote_copy(
            src_ref=src,
            dst_ref=dst,
            send_sem=self.send.at[k],
            recv_sem=self.recv.at[k],
            device_id=device,
            device_id_type=MESH,
        )
        made.start()
        self.started.append(made)
        return made


def kernel(
    prompt_ref, suffix_ref, q_ref, ku_ref, vu_ref, og_ref, fork_ref, length_ref,
    prompt_out, suffix_out, query_out, key_up_out, value_up_out,
    keys, keys_t, qry, qry_t, lgr, lgr_t, og_exp, qn_exp_t, bias, score, pgrad,
    acc_t, abs_t, sgrad_b, prob_b, kgrad, stat, stat_all,
    c1s, c1r, c2s, c2r, c3s, c3r,
    w1f, w1b, w1x, w1m, w1z, w1a, w2f, w2b, w2x, w2m, w2z, w2a,
    send_sem, recv_sem,
):
    ctx, sample = lax.axis_index("ctx"), lax.axis_index("sample")
    zl, x = ctx // X, ctx % X
    zh, y, core = sample // (Y * CORE), (sample // CORE) % Y, sample % CORE

    def at(zl_=zl, x_=x, zh_=zh, y_=y, core_=core):
        return (zl_ * X + x_, zh_ * (Y * CORE) + y_ * CORE + core_)

    sibling = at(core_=1 - core)

    def zh_by(d):
        return (zh + d + ZH) % ZH

    def y_by(d):
        return (y + d + Y) % Y

    def x_by(d):
        return (x + d + X) % X

    def zl_by(d):
        return (zl + d + ZL) % ZL

    sems = Sems(send_sem, recv_sem)

    partners = [sibling]
    partners += [at(zh_=zh_by(d)) for d in range(1, ZH)]
    partners += [at(y_=y_by(d)) for d in range(1, Y)]
    partners += [at(zl_=zl_by(a), x_=x_by(b)) for a in range(ZL) for b in range(X) if a + b]
    barrier = pltpu.get_barrier_semaphore()
    for device in partners:
        pl.semaphore_signal(barrier, inc=1, device_id=device, device_id_type=MESH)
    own = jnp.concatenate(
        [prompt_ref[0].astype(F32), prompt_ref[1].astype(F32), suffix_ref[0].astype(F32)], 0
    ).astype(BF16)
    keys[y, core, zh] = own
    pl.semaphore_wait(barrier, len(partners))

    from_zh = {}
    from_y = {}
    for d in (2, 1, 3):
        block = keys.at[y, core, zh]
        from_zh[d] = sems.copy(block, block, at(zh_=zh_by(d)))

    def spread_y(dz):
        block = keys.at[y, core, zh_by(-dz)]
        for d in (2, 1, 3):
            from_y[d, dz] = sems.copy(block, block, at(y_=y_by(d)))

    spread_y(0)

    lane = lax.broadcasted_iota(jnp.int32, (1, ROWS), 1)
    row_fork = (lane * 3277) >> 16
    row_step = (lane - row_fork * (RECOMP * HEADS)) >> 2

    def project(t, carry):
        rows = pl.ds(pl.multiple_of(t * TILE, TILE), TILE)
        q = q_ref[rows, :]
        og = og_ref[rows, :]
        head = lax.broadcasted_iota(jnp.int32, (TILE, NOPE), 0) & (HEADS - 1)
        q_nope = q[:, :NOPE]
        zero = jnp.zeros_like(q_nope)
        q_exp = jnp.concatenate([jnp.where(head == h, q_nope, zero) for h in range(HEADS)], 1)
        o_exp = jnp.concatenate([jnp.where(head == h, og, zero) for h in range(HEADS)], 1)
        og_exp[rows, :] = o_exp
        q_t = q_nope.T
        head_t = lax.broadcasted_iota(jnp.int32, (NOPE, TILE), 1) & (HEADS - 1)
        qn_exp_t[:, rows] = jnp.concatenate(
            [jnp.where(head_t == h, q_t, zero) for h in range(HEADS)], 0
        )
        whole = jnp.concatenate([dot(q_exp, ku_ref[...]).astype(BF16), q[:, NOPE:]], 1)
        qry[rows, :] = whole
        qry_t[:, rows] = whole.T
        grad = dot_nt(o_exp[:, :VHEAD], vu_ref[pl.ds(0, LATENT), :])
        for h in range(1, HEADS):
            grad += dot_nt(
                o_exp[:, h * VHEAD : (h + 1) * VHEAD], vu_ref[pl.ds(h * LATENT, LATENT), :]
            )
        grad = grad.astype(BF16)
        lgr[rows, :] = grad
        lgr_t[:, rows] = grad.T
        return carry

    lax.fori_loop(0, TILES, project, 0)

    for dz in (1, 3):
        from_zh[dz].wait_recv()
        spread_y(dz)

    def gather_rows(f, carry):
        limit, prompt = carry
        mine = row_fork == f
        return jnp.where(mine, length_ref[f], limit), jnp.where(mine, fork_ref[f], prompt)

    none = jnp.zeros((1, ROWS), jnp.int32)
    row_limit, row_prompt = lax.fori_loop(0, FORKS, gather_rows, (none, none))
    row_limit = row_limit - RECOMP + row_step
    first = jnp.broadcast_to(jnp.where(row_prompt == 0, 0.0, HIDDEN), (PKEYS, ROWS))
    second = jnp.broadcast_to(jnp.where(row_prompt == 1, 0.0, HIDDEN), (PKEYS, ROWS))
    position = ctx * SKEYS + lax.broadcasted_iota(jnp.int32, (SKEYS, ROWS), 0)

    def make_bias(b, carry):
        by, bc, bz = b // (CORE * ZH), (b // ZH) % CORE, b % ZH
        fork = bz * (Y * CORE) + by * CORE + bc
        last = jnp.where(row_fork == fork, row_limit, -1)
        seen = jnp.where(position <= last, 0.0, HIDDEN)
        bias[by, pl.ds(pl.multiple_of((bc * ZH + bz) * BLOCK, BLOCK), BLOCK), :] = (
            jnp.concatenate([first, second, seen], 0)
        )
        return carry

    lax.fori_loop(0, Y * CORE * ZH, make_bias, 0)

    from_zh[2].wait_recv()
    spread_y(2)

    from_core = {}

    def to_core(dy):
        part = keys.at[y_by(-dy), core]
        from_core[dy] = sems.copy(part, part, sibling)

    to_core(0)
    peak = jnp.full((1, ROWS), HIDDEN, F32)
    for i in range(Y):
        if i + 1 < Y:
            for dz in range(ZH):
                from_y[GRAY[i + 1], dz].wait_recv()
            to_core(GRAY[i + 1])
        from_core[GRAY[i]].wait_recv()
        part = y_by(-GRAY[i])
        tile = keys[part].reshape(KEYS, WIDTH)
        s = dot(tile, qry_t[...]) + bias[part]
        score[part] = s
        peak = jnp.maximum(peak, jnp.max(s, 0, keepdims=True))
        pgrad[part] = dot(tile[:, :LATENT], lgr_t[...])
        keys_t[part] = tile.T

    def exponents(part, carry):
        total, delta = carry
        p = jnp.exp((score[part] - peak) * SCALE)
        score[part] = p
        total = total + jnp.sum(p, 0, keepdims=True)
        delta = delta + jnp.sum(p * pgrad[part], 0, keepdims=True)
        return total, delta

    zeros = jnp.zeros((1, ROWS), F32)
    total, delta = lax.fori_loop(0, Y, exponents, (zeros, zeros))

    for t in range(TILES):
        cols = slice(t * TILE, (t + 1) * TILE)
        stat[t : t + 1, :] = peak[:, cols]
        stat[TILES + t : TILES + t + 1, :] = total[:, cols]
        stat[2 * TILES + t : 2 * TILES + t + 1, :] = delta[:, cols]
    stat[3 * TILES : 3 * TILES + 1, :] = jnp.zeros((1, TILE), F32)
    stat_copies = []
    for a in range(ZL):
        for b in range(X):
            if a + b:
                stat_copies.append(
                    sems.copy(stat, stat_all.at[ctx], at(zl_=zl_by(a), x_=x_by(b)))
                )
    stat_all[ctx] = stat[...]

    acc_t[...] = jnp.zeros_like(acc_t)

    def weigh(part, carry):
        acc_t[...] += dot(keys_t[part, :LATENT, :], score[part].astype(BF16))
        return carry

    lax.fori_loop(0, Y, weigh, 0)

    for made in stat_copies:
        made.wait_recv()
    all_peak = stat_all[:, 0:TILES, :]
    top = jnp.max(all_peak, 0)
    shrink = jnp.exp((all_peak - top[None]) * SCALE)
    whole_total = jnp.sum(stat_all[:, TILES : 2 * TILES, :] * shrink, 0)
    whole_delta = jnp.sum(stat_all[:, 2 * TILES : 3 * TILES, :] * shrink, 0)
    inverse = 1.0 / whole_total
    weight = jnp.exp((stat[0:TILES, :] - top) * SCALE) * inverse
    row_delta = whole_delta * inverse

    def as_row(v):
        return jnp.concatenate([v[t : t + 1, :] for t in range(TILES)], 1)

    weight, row_delta = as_row(weight), as_row(row_delta)

    def send_x(src, dst):
        return [
            sems.copy(src.at[x_by(d)], dst.at[d - 1], at(x_=x_by(d))) for d in (2, 1, 3)
        ]

    scaled = (acc_t[...] * weight).astype(BF16)
    for h in range(HEADS):
        cols = slice(h * VHEAD, (h + 1) * VHEAD)
        part = dot(scaled, og_exp[:, cols]).reshape(ZL, W1, TILE)
        w1f[h] = part
        w1b[h] = part.astype(BF16)
    w1_x = send_x(w1b, w1x)

    abs_t[...] = jnp.zeros_like(abs_t)

    def grads(part, carry):
        p = score[part] * weight
        prob_b[part] = p.astype(BF16)
        sg = (p * (pgrad[part] - row_delta) * SCALE).astype(BF16)
        sgrad_b[part] = sg
        abs_t[...] += dot(keys_t[part], sg)
        return carry

    lax.fori_loop(0, Y, grads, 0)

    lat = abs_t[:LATENT, :].astype(BF16)
    kup = dot_nt(qn_exp_t[...], lat)
    for b in range(LATENT // TILE):
        w2f[b * 512 : (b + 1) * 512, :] = kup[:, b * TILE : (b + 1) * TILE]
    spread = dot(ku_ref[...], lat)
    head_of = lane & (HEADS - 1)
    nope = jnp.zeros((NOPE, ROWS), F32)
    for h in range(HEADS):
        nope = jnp.where(head_of == h, spread[h * NOPE : (h + 1) * NOPE, :], nope)
    for t in range(TILES):
        cols = slice(t * TILE, (t + 1) * TILE)
        base = 2048 + t * QUERY
        w2f[base : base + NOPE, :] = nope[:, cols]
        w2f[base + NOPE : base + QUERY, :] = abs_t[LATENT:WIDTH, cols]
    w2f[2048 + TILES * QUERY : 3072, :] = jnp.zeros((64, TILE), F32)
    w2b[...] = w2f[...].reshape(X, ZL, W2, TILE).astype(BF16)
    w2_x = send_x(w2b, w2x)

    from_core2 = {}
    for i in (1, 2, 3, 0):
        part = y_by(i)
        grad = dot(sgrad_b[part], qry[...])
        value = dot(prob_b[part], lgr[...])
        kgrad[part, :, :, :LATENT] = (grad[:, :LATENT] + value).reshape(
            CORE, ZH * BLOCK, LATENT
        )
        kgrad[part, :, :, LATENT:] = grad[:, LATENT:].reshape(CORE, ZH * BLOCK, ROPE)
        c1s[part] = kgrad[part, 1 - core].astype(BF16)
        from_core2[i] = sems.copy(c1s.at[part], c1r.at[part], sibling)

    def sum_x(made, full, came, middle):
        for m in made:
            m.wait_recv()
        add = full + came[0].astype(F32) + came[1].astype(F32) + came[2].astype(F32)
        middle[...] = add.astype(BF16)

    def send_zl(middle, dst):
        return [
            sems.copy(middle.at[zl_by(d)], dst.at[d - 1], at(zl_=zl_by(d))) for d in (2, 1, 3)
        ]

    sum_x(w1_x, w1f[x], w1x, w1m)
    w1_z = send_zl(w1m, w1z)

    from_y2 = []
    for i in (1, 2, 3):
        part = y_by(i)
        from_core2[i].wait_recv()
        c2s[i - 1] = (kgrad[part, core] + c1r[part].astype(F32)).astype(BF16)
        from_y2.append(sems.copy(c2s.at[i - 1], c2r.at[i - 1], at(y_=part)))

    own_rows = pl.ds(pl.multiple_of(x * (ZL * W2), W2), ZL * W2)
    sum_x(w2_x, w2f[own_rows, :].reshape(ZL, W2, TILE), w2x, w2m)
    w2_z = send_zl(w2m, w2z)

    from_core2[0].wait_recv()
    for made in from_y2:
        made.wait_recv()
    mine = kgrad[y, core] + c1r[y].astype(F32)
    for i in range(Y - 1):
        mine += c2r[i].astype(F32)
    kgrad[y, core] = mine
    c3s[...] = mine.reshape(ZH, BLOCK, WIDTH).astype(BF16)
    from_zh2 = [sems.copy(c3s.at[zh_by(d)], c3r.at[d - 1], at(zh_=zh_by(d))) for d in (2, 1, 3)]

    def sum_zl(made, middle, came, whole):
        for m in made:
            m.wait_recv()
        add = middle[zl].astype(F32)
        for i in range(ZL - 1):
            add += came[i].astype(F32)
        whole[x, zl] = add.astype(BF16)
        block = whole.at[x, zl]
        return [sems.copy(block, block, at(zl_=zl_by(d))) for d in (2, 1, 3)]

    def gather_x(made, whole):
        for m in made:
            m.wait_recv()
        block = whole.at[x]
        return [sems.copy(block, block, at(x_=x_by(d))) for d in (2, 1, 3)]

    w1_z = sum_zl(w1_z, w1m, w1z, w1a)
    w2_z = sum_zl(w2_z, w2m, w2z, w2a)
    w1_x = gather_x(w1_z, w1a)
    w2_x = gather_x(w2_z, w2a)

    for made in from_zh2:
        made.wait_recv()
    final = kgrad[y, core, pl.ds(pl.multiple_of(zh * BLOCK, BLOCK), BLOCK), :]
    for i in range(ZH - 1):
        final += c3r[i].astype(F32)
    prompt_out[0] = final[:PKEYS]
    prompt_out[1] = final[PKEYS : 2 * PKEYS]
    suffix_out[0] = final[2 * PKEYS :]

    for made in w1_x:
        made.wait_recv()
    value_up_out[...] = w1a[...].reshape(HEADS * LATENT, VHEAD).astype(F32)
    for made in w2_x:
        made.wait_recv()
    w2f[...] = w2a[...].reshape(3072, TILE).astype(F32)
    for b in range(LATENT // TILE):
        key_up_out[:, b * TILE : (b + 1) * TILE] = w2f[b * 512 : (b + 1) * 512, :]
    for t in range(TILES):
        base = 2048 + t * QUERY
        query_out[t * TILE : (t + 1) * TILE, :] = w2f[base : base + QUERY, :].T
    for made in sems.started:
        made.wait_send()


def shards(prompt, suffix, queries, key_up, value_up, out_grad, fork_prompt, suffix_length):
    vmem = pl.BlockSpec(memory_space=pltpu.VMEM)
    smem = pl.BlockSpec(memory_space=pltpu.SMEM)
    copies = 96
    outs = pl.pallas_call(
        kernel,
        out_shape=(
            jax.ShapeDtypeStruct((2, PKEYS, WIDTH), F32),
            jax.ShapeDtypeStruct((1, SKEYS, WIDTH), F32),
            jax.ShapeDtypeStruct((ROWS, QUERY), F32),
            jax.ShapeDtypeStruct((HEADS * NOPE, LATENT), F32),
            jax.ShapeDtypeStruct((HEADS * LATENT, VHEAD), F32),
        ),
        in_specs=[vmem] * 6 + [smem] * 2,
        out_specs=(vmem,) * 5,
        scratch_shapes=[
            pltpu.VMEM((Y, CORE, ZH, BLOCK, WIDTH), BF16),
            pltpu.VMEM((Y, WIDTH, KEYS), BF16),
            pltpu.VMEM((ROWS, WIDTH), BF16),
            pltpu.VMEM((WIDTH, ROWS), BF16),
            pltpu.VMEM((ROWS, LATENT), BF16),
            pltpu.VMEM((LATENT, ROWS), BF16),
            pltpu.VMEM((ROWS, HEADS * VHEAD), BF16),
            pltpu.VMEM((HEADS * NOPE, ROWS), BF16),
            pltpu.VMEM((Y, KEYS, ROWS), F32),
            pltpu.VMEM((Y, KEYS, ROWS), F32),
            pltpu.VMEM((Y, KEYS, ROWS), F32),
            pltpu.VMEM((LATENT, ROWS), F32),
            pltpu.VMEM((WIDTH, ROWS), F32),
            pltpu.VMEM((Y, KEYS, ROWS), BF16),
            pltpu.VMEM((Y, KEYS, ROWS), BF16),
            pltpu.VMEM((Y, CORE, ZH * BLOCK, WIDTH), F32),
            pltpu.VMEM((16, TILE), F32),
            pltpu.VMEM((ZL * X, 16, TILE), F32),
            pltpu.VMEM((Y, ZH * BLOCK, WIDTH), BF16),
            pltpu.VMEM((Y, ZH * BLOCK, WIDTH), BF16),
            pltpu.VMEM((Y - 1, ZH * BLOCK, WIDTH), BF16),
            pltpu.VMEM((Y - 1, ZH * BLOCK, WIDTH), BF16),
            pltpu.VMEM((ZH, BLOCK, WIDTH), BF16),
            pltpu.VMEM((ZH - 1, BLOCK, WIDTH), BF16),
            pltpu.VMEM((X, ZL, W1, TILE), F32),
            pltpu.VMEM((X, ZL, W1, TILE), BF16),
            pltpu.VMEM((X - 1, ZL, W1, TILE), BF16),
            pltpu.VMEM((ZL, W1, TILE), BF16),
            pltpu.VMEM((ZL - 1, W1, TILE), BF16),
            pltpu.VMEM((X, ZL, W1, TILE), BF16),
            pltpu.VMEM((X * ZL * W2, TILE), F32),
            pltpu.VMEM((X, ZL, W2, TILE), BF16),
            pltpu.VMEM((X - 1, ZL, W2, TILE), BF16),
            pltpu.VMEM((ZL, W2, TILE), BF16),
            pltpu.VMEM((ZL - 1, W2, TILE), BF16),
            pltpu.VMEM((X, ZL, W2, TILE), BF16),
            pltpu.SemaphoreType.DMA((copies,)),
            pltpu.SemaphoreType.DMA((copies,)),
        ],
        compiler_params=pltpu.CompilerParams(
            collective_id=0, has_side_effects=True, vmem_limit_bytes=52 << 20
        ),
        cost_estimate=pl.CostEstimate(
            flops=8_000_000_000, bytes_accessed=6_000_000, transcendentals=700_000
        ),
        name="latent_backward",
    )(
        prompt,
        suffix,
        queries.reshape(ROWS, QUERY),
        key_up.reshape(HEADS * NOPE, LATENT),
        value_up.reshape(HEADS * LATENT, VHEAD),
        out_grad.reshape(ROWS, VHEAD),
        fork_prompt,
        suffix_length,
    )
    prompt_grad, suffix_grad, query_grad, key_up_grad, value_up_grad = outs
    return (
        prompt_grad,
        suffix_grad,
        query_grad.reshape(FORKS, RECOMP, HEADS, QUERY),
        key_up_grad.reshape(HEADS, NOPE, LATENT),
        value_up_grad.reshape(HEADS, LATENT, VHEAD),
    )


def solution(mesh):
    return jax.shard_map(
        shards,
        mesh=mesh,
        in_specs=(
            P(None, ("ctx", "sample"), None),
            P("sample", "ctx", None),
            P(None, None, "sample", None),
            P("sample", None, None),
            P("sample", None, None),
            P(None, None, "sample", None),
            P(),
            P(),
        ),
        out_specs=(
            P(None, ("ctx", "sample"), None),
            P("sample", "ctx", None),
            P(None, None, "sample", None),
            P("sample", None, None),
            P("sample", None, None),
        ),
        check_vma=False,
    )
```

time: 1080 us -> 106 us (0.10)
  the two profiles are of different devices: /device:TPU:6 before, /device:TPU:1 now
where the time goes in v1:
time: 106 us
  Pallas kernels  96 us (91%)
  local copies, waits for them, and re-layouts  9.2 us (9%)
    pallas_call x1, Pallas kernels, shards(): pl.pallas_call(kernel, out_shape=(jax.ShapeDtypeStruct((2, PKEYS, WIDTH),...  96 us
    unnamed x22, local copies, waits for them, and re-layouts  5.78 us
    reshape x1, local copies, waits for them, and re-layouts, shards(): query_grad.reshape(FORKS, RECOMP, HEADS, QUERY)  2.2 us

profile of v1, /device:TPU:1, one launch (start us, length us, event | category | flops | bytes accessed | tf_op | source)
XLA Modules:
  0.0 106.0 jit_solution(14409182528517184363)
XLA Ops:
  0.6 0.0 copy-start
  0.6 0.0 copy-start.3
  0.7 0.0 copy-start.4
  0.7 0.0 copy-start.5
  0.7 0.0 copy-start.6
  0.7 1.2 %reshape.31.q_ref = bf16[640,192]{1,0:T(8,128)(2,1)S(1)} reshape(bf16[32,5,4,192]{3,2,1,0:T(4,128)(2,1)} %param.10) | data formatting | bytes 491520 | tf_op jit(solution)/shard_map/reshape | solution.py:455
  1.9 0.0 copy-done
  1.9 0.0 copy-done.3
  1.9 0.0 copy-done.4
  1.9 0.0 copy-done.5
  1.9 0.0 copy-done.6
  2.0 0.0 copy-start.1
  2.0 1.0 copy-done.1
  3.0 0.0 copy-start.2
  3.0 0.9 copy-done.2
  3.9 96.0 %latent_backward.1 = (f32[2,8,576]{2,1,0:T(8,128)S(1)}, f32[1,16,576]{2,1,0:T(8,128)S(1)}, f32[640,192]{1,0:T(8,128)}, f32[512,512]{1,0:T(8,128)}, f32[2048,128]{1,0:T(8,128)}) custom-call(bf16[2,8,576]{2,1,0:T(8,128)(2,1)S(1)} %copy-done.3, bf16[1,16,576]{2,1,0:T(8,128)(2,1)S(1)} %copy-done.4, bf16[640,192]{1,0:T(8,128)(2,1)S(1)} %reshape.31.q_ref, ...), custom_call_target="tpu_custom_call" | custom-call | flops 8000000000 | bytes 6000000 | tf_op jit(solution)/shard_map/latent_backward/pallas_call | solution.py:394
  99.9 0.0 copy-start.8
  99.9 2.2 %reshape.35 = f32[32,5,4,192]{3,2,1,0:T(4,128)} reshape(f32[640,192]{1,0:T(8,128)} %get-tuple-element.12) | data formatting | bytes 983040 | tf_op jit(solution)/shard_map/reshape | solution.py:466
  102.1 0.6 copy.17
  102.8 0.6 copy.18
  103.4 0.0 copy-done.8
  103.4 0.0 copy-start.7
  103.4 1.0 copy.19
  104.3 0.6 copy-done.7
  105.0 1.0 copy.20
Async XLA Ops:
  0.6 1.3 %copy-start = (bf16[4,128,512]{2,1,0:T(8,128)(2,1)S(1)}, bf16[4,128,512]{2,1,0:T(8,128)(2,1)}, u32[]{:S(2)}) copy-start(bf16[4,128,512]{2,1,0:T(8,128)(2,1)} %param.11) | copy-start | bytes 1572868
  0.6 1.3 %copy-start.3 = (bf16[2,8,576]{2,1,0:T(8,128)(2,1)S(1)}, bf16[2,8,576]{2,1,0:T(8,128)(2,1)}, u32[]{:S(2)}) copy-start(bf16[2,8,576]{2,1,0:T(8,128)(2,1)} %prompt_ref.1) | copy-start | bytes 55300
  0.7 1.3 %copy-start.4 = (bf16[1,16,576]{2,1,0:T(8,128)(2,1)S(1)}, bf16[1,16,576]{2,1,0:T(8,128)(2,1)}, u32[]{:S(2)}) copy-start(bf16[1,16,576]{2,1,0:T(8,128)(2,1)} %suffix_ref.1) | copy-start | bytes 55300
  0.7 1.3 %copy-start.5 = (s32[32]{0:T(128)S(1)}, s32[32]{0:T(128)}, u32[]{:S(2)}) copy-start(s32[32]{0:T(128)} %fork_ref.1) | copy-start | bytes 388
  0.7 1.3 %copy-start.6 = (s32[32]{0:T(128)S(1)}, s32[32]{0:T(128)}, u32[]{:S(2)}) copy-start(s32[32]{0:T(128)} %length_ref.1) | copy-start | bytes 388
  2.0 1.0 copy-start.1
  3.0 0.9 copy-start.2
  99.9 3.4 %copy-start.8 = (f32[512,512]{1,0:T(8,128)S(1)}, f32[512,512]{1,0:T(8,128)}, u32[]{:S(2)}) copy-start(f32[512,512]{1,0:T(8,128)} %get-tuple-element.13) | copy-start | bytes 3145732
  103.4 1.6 %copy-start.7 = (f32[2048,128]{1,0:T(8,128)S(1)}, f32[2048,128]{1,0:T(8,128)}, u32[]{:S(2)}) copy-start(f32[2048,128]{1,0:T(8,128)} %get-tuple-element.14) | copy-start | bytes 3145732

commit v2 on v1

--- a/solution.py
+++ b/solution.py
@@ -22,11 +22,10 @@
 TILES = ROWS // TILE
 PKEYS, SKEYS = 8, 16
 BLOCK = 2 * PKEYS + SKEYS
-KEYS = CORE * ZH * BLOCK
+KEYS = CORE * Y * BLOCK
 SCALE = QUERY**-0.5
 W1 = HEADS * LATENT // 16
 W2 = 192
-GRAY = (0, 1, 3, 2)
 
 
 def dot(a, b):
@@ -60,9 +59,8 @@
 def kernel(
     prompt_ref, suffix_ref, q_ref, ku_ref, vu_ref, og_ref, fork_ref, length_ref,
     prompt_out, suffix_out, query_out, key_up_out, value_up_out,
-    keys, keys_t, qry, qry_t, lgr, lgr_t, og_exp, qn_exp_t, bias, score, pgrad,
-    acc_t, abs_t, sgrad_b, prob_b, kgrad, stat, stat_all,
-    c1s, c1r, c2s, c2r, c3s, c3r,
+    keys, qry, qry_t, lgr, lgr_t, og_exp, qn_exp_t, bias, score, pgrad, peaks,
+    acc_t, dif_t, kgrad, stat, stat_all, c1s, c1r, c2s, c2r, c3s, c3r,
     w1f, w1b, w1x, w1m, w1z, w1a, w2f, w2b, w2x, w2m, w2z, w2a,
     send_sem, recv_sem,
 ):
@@ -99,19 +97,27 @@
     own = jnp.concatenate(
         [prompt_ref[0].astype(F32), prompt_ref[1].astype(F32), suffix_ref[0].astype(F32)], 0
     ).astype(BF16)
-    keys[y, core, zh] = own
+    keys[zh, core, y] = own
     pl.semaphore_wait(barrier, len(partners))
 
     from_zh = {}
     from_y = {}
+    from_core = {}
     for d in (2, 1, 3):
-        block = keys.at[y, core, zh]
+        block = keys.at[zh, core, y]
         from_zh[d] = sems.copy(block, block, at(zh_=zh_by(d)))
 
     def spread_y(dz):
-        block = keys.at[y, core, zh_by(-dz)]
-        for d in (2, 1, 3):
-            from_y[d, dz] = sems.copy(block, block, at(y_=y_by(d)))
+        if dz:
+            from_zh[dz].wait_recv()
+        block = keys.at[zh_by(-dz), core, y]
+        from_y[dz] = [sems.copy(block, block, at(y_=y_by(d))) for d in (2, 1, 3)]
+
+    def to_core(dz):
+        for made in from_y[dz]:
+            made.wait_recv()
+        part = keys.at[zh_by(-dz), core]
+        from_core[dz] = sems.copy(part, part, sibling)
 
     spread_y(0)
 
@@ -149,10 +155,6 @@
 
     lax.fori_loop(0, TILES, project, 0)
 
-    for dz in (1, 3):
-        from_zh[dz].wait_recv()
-        spread_y(dz)
-
     def gather_rows(f, carry):
         limit, prompt = carry
         mine = row_fork == f
@@ -166,53 +168,75 @@
     position = ctx * SKEYS + lax.broadcasted_iota(jnp.int32, (SKEYS, ROWS), 0)
 
     def make_bias(b, carry):
-        by, bc, bz = b // (CORE * ZH), (b // ZH) % CORE, b % ZH
+        bz, bc, by = b // (CORE * Y), (b // Y) % CORE, b % Y
         fork = bz * (Y * CORE) + by * CORE + bc
         last = jnp.where(row_fork == fork, row_limit, -1)
         seen = jnp.where(position <= last, 0.0, HIDDEN)
-        bias[by, pl.ds(pl.multiple_of((bc * ZH + bz) * BLOCK, BLOCK), BLOCK), :] = (
+        bias[bz, pl.ds(pl.multiple_of((bc * Y + by) * BLOCK, BLOCK), BLOCK), :] = (
             jnp.concatenate([first, second, seen], 0)
         )
         return carry
 
+    to_core(0)
     lax.fori_loop(0, Y * CORE * ZH, make_bias, 0)
 
-    from_zh[2].wait_recv()
-    spread_y(2)
-
-    from_core = {}
-
-    def to_core(dy):
-        part = keys.at[y_by(-dy), core]
-        from_core[dy] = sems.copy(part, part, sibling)
-
-    to_core(0)
-    peak = jnp.full((1, ROWS), HIDDEN, F32)
-    for i in range(Y):
-        if i + 1 < Y:
-            for dz in range(ZH):
-                from_y[GRAY[i + 1], dz].wait_recv()
-            to_core(GRAY[i + 1])
-        from_core[GRAY[i]].wait_recv()
-        part = y_by(-GRAY[i])
+    def scores_of(dz):
+        from_core[dz].wait_recv()
+        part = zh_by(-dz)
         tile = keys[part].reshape(KEYS, WIDTH)
         s = dot(tile, qry_t[...]) + bias[part]
-        score[part] = s
-        peak = jnp.maximum(peak, jnp.max(s, 0, keepdims=True))
-        pgrad[part] = dot(tile[:, :LATENT], lgr_t[...])
-        keys_t[part] = tile.T
-
-    def exponents(part, carry):
-        total, delta = carry
-        p = jnp.exp((score[part] - peak) * SCALE)
+        peak = jnp.max(s, 0, keepdims=True)
+        p = jnp.exp((s - peak) * SCALE)
         score[part] = p
-        total = total + jnp.sum(p, 0, keepdims=True)
-        delta = delta + jnp.sum(p * pgrad[part], 0, keepdims=True)
-        return total, delta
-
-    zeros = jnp.zeros((1, ROWS), F32)
-    total, delta = lax.fori_loop(0, Y, exponents, (zeros, zeros))
-
+        grad = dot(tile[:, :LATENT], lgr_t[...])
+        pgrad[part] = grad
+        total = jnp.sum(p, 0, keepdims=True)
+        mean = jnp.sum(p * grad, 0, keepdims=True) / total
+        peaks[dz] = peak
+        return part, peak, total, mean
+
+    def merged(left, right):
+        top = jnp.maximum(left[0], right[0])
+        shrink_left = jnp.exp((left[0] - top) * SCALE)
+        shrink_right = jnp.exp((right[0] - top) * SCALE)
+        total_left, total_right = left[1] * shrink_left, right[1] * shrink_right
+        total = total_left + total_right
+        mean = (total_left * left[2] + total_right * right[2]) / total
+        return (top, total, mean), shrink_left, shrink_right
+
+    def sums_of(part, mean):
+        tile_t = keys[part].reshape(KEYS, WIDTH).T
+        p = score[part]
+        return dot(tile_t, p.astype(BF16)), dot(
+            tile_t, (p * (pgrad[part] - mean)).astype(BF16)
+        )
+
+    def add_sums(state, new, part):
+        both, shrink_left, shrink_right = merged(state, new)
+        acc, grad = sums_of(part, new[2])
+        old = acc_t[...]
+        acc_t[...] = shrink_left * old + shrink_right * acc
+        dif_t[...] = shrink_left * (dif_t[...] + (state[2] - both[2]) * old) + shrink_right * (
+            grad + (new[2] - both[2]) * acc
+        )
+        return both
+
+    part, *state = scores_of(0)
+    spread_y(1)
+    spread_y(3)
+    acc_t[...], dif_t[...] = sums_of(part, state[2])
+    to_core(1)
+    to_core(3)
+    spread_y(2)
+    part, *new = scores_of(1)
+    state = add_sums(state, new, part)
+    to_core(2)
+    part, *new = scores_of(3)
+    state = add_sums(state, new, part)
+    part, *new = scores_of(2)
+    (peak, total, mean), _, _ = merged(state, new)
+
+    delta = mean * total
     for t in range(TILES):
         cols = slice(t * TILE, (t + 1) * TILE)
         stat[t : t + 1, :] = peak[:, cols]
@@ -228,13 +252,7 @@
                 )
     stat_all[ctx] = stat[...]
 
-    acc_t[...] = jnp.zeros_like(acc_t)
-
-    def weigh(part, carry):
-        acc_t[...] += dot(keys_t[part, :LATENT, :], score[part].astype(BF16))
-        return carry
-
-    lax.fori_loop(0, Y, weigh, 0)
+    add_sums(state, new, part)
 
     for made in stat_copies:
         made.wait_recv()
@@ -244,20 +262,25 @@
     whole_total = jnp.sum(stat_all[:, TILES : 2 * TILES, :] * shrink, 0)
     whole_delta = jnp.sum(stat_all[:, 2 * TILES : 3 * TILES, :] * shrink, 0)
     inverse = 1.0 / whole_total
-    weight = jnp.exp((stat[0:TILES, :] - top) * SCALE) * inverse
-    row_delta = whole_delta * inverse
 
     def as_row(v):
         return jnp.concatenate([v[t : t + 1, :] for t in range(TILES)], 1)
 
-    weight, row_delta = as_row(weight), as_row(row_delta)
+    top, inverse, row_delta = as_row(top), as_row(inverse), as_row(whole_delta * inverse)
+    weight = jnp.exp((peak - top) * SCALE) * inverse
 
     def send_x(src, dst):
-        return [
-            sems.copy(src.at[x_by(d)], dst.at[d - 1], at(x_=x_by(d))) for d in (2, 1, 3)
-        ]
-
-    scaled = (acc_t[...] * weight).astype(BF16)
+        made = {}
+        for e in (2, 1, 3, 0):
+            made[e] = [
+                sems.copy(
+                    src.at[x_by(d), zl_by(e)], dst.at[d - 1, zl_by(e)], at(x_=x_by(d))
+                )
+                for d in (2, 1, 3)
+            ]
+        return made
+
+    scaled = (acc_t[:LATENT, :] * weight).astype(BF16)
     for h in range(HEADS):
         cols = slice(h * VHEAD, (h + 1) * VHEAD)
         part = dot(scaled, og_exp[:, cols]).reshape(ZL, W1, TILE)
@@ -265,19 +288,10 @@
         w1b[h] = part.astype(BF16)
     w1_x = send_x(w1b, w1x)
 
-    abs_t[...] = jnp.zeros_like(abs_t)
-
-    def grads(part, carry):
-        p = score[part] * weight
-        prob_b[part] = p.astype(BF16)
-        sg = (p * (pgrad[part] - row_delta) * SCALE).astype(BF16)
-        sgrad_b[part] = sg
-        abs_t[...] += dot(keys_t[part], sg)
-        return carry
-
-    lax.fori_loop(0, Y, grads, 0)
-
-    lat = abs_t[:LATENT, :].astype(BF16)
+    shift = row_delta - mean
+    factor = weight * SCALE
+    lat = (factor * (dif_t[:LATENT, :] - shift * acc_t[:LATENT, :])).astype(BF16)
+    rope = factor * (dif_t[LATENT:, :] - shift * acc_t[LATENT:, :])
     kup = dot_nt(qn_exp_t[...], lat)
     for b in range(LATENT // TILE):
         w2f[b * 512 : (b + 1) * 512, :] = kup[:, b * TILE : (b + 1) * TILE]
@@ -290,57 +304,61 @@
         cols = slice(t * TILE, (t + 1) * TILE)
         base = 2048 + t * QUERY
         w2f[base : base + NOPE, :] = nope[:, cols]
-        w2f[base + NOPE : base + QUERY, :] = abs_t[LATENT:WIDTH, cols]
+        w2f[base + NOPE : base + QUERY, :] = rope[:, cols]
     w2f[2048 + TILES * QUERY : 3072, :] = jnp.zeros((64, TILE), F32)
     w2b[...] = w2f[...].reshape(X, ZL, W2, TILE).astype(BF16)
     w2_x = send_x(w2b, w2x)
 
-    from_core2 = {}
-    for i in (1, 2, 3, 0):
-        part = y_by(i)
-        grad = dot(sgrad_b[part], qry[...])
-        value = dot(prob_b[part], lgr[...])
-        kgrad[part, :, :, :LATENT] = (grad[:, :LATENT] + value).reshape(
-            CORE, ZH * BLOCK, LATENT
-        )
-        kgrad[part, :, :, LATENT:] = grad[:, LATENT:].reshape(CORE, ZH * BLOCK, ROPE)
+    core_sums, y_sums, zh_sums = {}, {}, {}
+
+    def key_grads(dz):
+        part = zh_by(-dz)
+        p = score[part] * (jnp.exp((peaks[dz] - top) * SCALE) * inverse)
+        sg = (p * (pgrad[part] - row_delta) * SCALE).astype(BF16)
+        grad = dot(sg, qry[...])
+        value = dot(p.astype(BF16), lgr[...])
+        kgrad[part, :, :, :LATENT] = (grad[:, :LATENT] + value).reshape(CORE, Y * BLOCK, LATENT)
+        kgrad[part, :, :, LATENT:] = grad[:, LATENT:].reshape(CORE, Y * BLOCK, ROPE)
         c1s[part] = kgrad[part, 1 - core].astype(BF16)
-        from_core2[i] = sems.copy(c1s.at[part], c1r.at[part], sibling)
-
-    def sum_x(made, full, came, middle):
-        for m in made:
-            m.wait_recv()
-        add = full + came[0].astype(F32) + came[1].astype(F32) + came[2].astype(F32)
-        middle[...] = add.astype(BF16)
-
-    def send_zl(middle, dst):
-        return [
-            sems.copy(middle.at[zl_by(d)], dst.at[d - 1], at(zl_=zl_by(d))) for d in (2, 1, 3)
+        core_sums[dz] = sems.copy(c1s.at[part], c1r.at[part], sibling)
+
+    def add_cores(dz):
+        part = zh_by(-dz)
+        core_sums[dz].wait_recv()
+        both = kgrad[part, core] + c1r[part].astype(F32)
+        kgrad[part, core] = both
+        c2s[dz] = both.reshape(Y, BLOCK, WIDTH).astype(BF16)
+        y_sums[dz] = [
+            sems.copy(c2s.at[dz, y_by(d)], c2r.at[dz, d - 1], at(y_=y_by(d))) for d in (2, 1, 3)
         ]
 
-    sum_x(w1_x, w1f[x], w1x, w1m)
-    w1_z = send_zl(w1m, w1z)
-
-    from_y2 = []
-    for i in (1, 2, 3):
-        part = y_by(i)
-        from_core2[i].wait_recv()
-        c2s[i - 1] = (kgrad[part, core] + c1r[part].astype(F32)).astype(BF16)
-        from_y2.append(sems.copy(c2s.at[i - 1], c2r.at[i - 1], at(y_=part)))
-
-    own_rows = pl.ds(pl.multiple_of(x * (ZL * W2), W2), ZL * W2)
-    sum_x(w2_x, w2f[own_rows, :].reshape(ZL, W2, TILE), w2x, w2m)
-    w2_z = send_zl(w2m, w2z)
-
-    from_core2[0].wait_recv()
-    for made in from_y2:
-        made.wait_recv()
-    mine = kgrad[y, core] + c1r[y].astype(F32)
-    for i in range(Y - 1):
-        mine += c2r[i].astype(F32)
-    kgrad[y, core] = mine
-    c3s[...] = mine.reshape(ZH, BLOCK, WIDTH).astype(BF16)
-    from_zh2 = [sems.copy(c3s.at[zh_by(d)], c3r.at[d - 1], at(zh_=zh_by(d))) for d in (2, 1, 3)]
+    def add_ys(dz):
+        for made in y_sums[dz]:
+            made.wait_recv()
+        rows = pl.ds(pl.multiple_of(y * BLOCK, BLOCK), BLOCK)
+        mine = kgrad[zh_by(-dz), core, rows, :]
+        for i in range(Y - 1):
+            mine += c2r[dz, i].astype(F32)
+        if dz == 0:
+            return mine
+        c3s[dz - 1] = mine.astype(BF16)
+        zh_sums[dz] = sems.copy(c3s.at[dz - 1], c3r.at[dz - 1], at(zh_=zh_by(-dz)))
+
+    def sum_x(made, full, came, middle, dst):
+        out = []
+        for e in (2, 1, 3, 0):
+            for m in made[e]:
+                m.wait_recv()
+            to = zl_by(e)
+            add = full(to) + came[0, to].astype(F32) + came[1, to].astype(F32)
+            middle[to] = (add + came[2, to].astype(F32)).astype(BF16)
+            if e:
+                out.append(sems.copy(middle.at[to], dst.at[e - 1], at(zl_=to)))
+        return out
+
+    def spread_x(whole, e):
+        block = whole.at[x, zl_by(-e)]
+        return [sems.copy(block, block, at(x_=x_by(d))) for d in (2, 1, 3)]
 
     def sum_zl(made, middle, came, whole):
         for m in made:
@@ -350,24 +368,39 @@
             add += came[i].astype(F32)
         whole[x, zl] = add.astype(BF16)
         block = whole.at[x, zl]
-        return [sems.copy(block, block, at(zl_=zl_by(d))) for d in (2, 1, 3)]
-
-    def gather_x(made, whole):
-        for m in made:
-            m.wait_recv()
-        block = whole.at[x]
-        return [sems.copy(block, block, at(x_=x_by(d))) for d in (2, 1, 3)]
-
-    w1_z = sum_zl(w1_z, w1m, w1z, w1a)
-    w2_z = sum_zl(w2_z, w2m, w2z, w2a)
-    w1_x = gather_x(w1_z, w1a)
-    w2_x = gather_x(w2_z, w2a)
-
-    for made in from_zh2:
-        made.wait_recv()
-    final = kgrad[y, core, pl.ds(pl.multiple_of(zh * BLOCK, BLOCK), BLOCK), :]
-    for i in range(ZH - 1):
-        final += c3r[i].astype(F32)
+        back = {e: sems.copy(block, block, at(zl_=zl_by(e))) for e in (2, 1, 3)}
+        return back, spread_x(whole, 0)
+
+    def gather_x(back, out, whole):
+        for e in (1, 3, 2):
+            back[e].wait_recv()
+            out += spread_x(whole, e)
+
+    def w2_rows(to):
+        return w2f[pl.ds(pl.multiple_of((x * ZL + to) * W2, W2), W2), :]
+
+    key_grads(2)
+    key_grads(1)
+    add_cores(2)
+    key_grads(3)
+    add_cores(1)
+    key_grads(0)
+    w1_z = sum_x(w1_x, lambda to: w1f[x, to], w1x, w1m, w1z)
+    add_cores(3)
+    add_ys(2)
+    w2_z = sum_x(w2_x, w2_rows, w2x, w2m, w2z)
+    add_ys(1)
+    add_ys(3)
+    add_cores(0)
+    w1_back, w1_x = sum_zl(w1_z, w1m, w1z, w1a)
+    final = add_ys(0)
+    w2_back, w2_x = sum_zl(w2_z, w2m, w2z, w2a)
+    gather_x(w1_back, w1_x, w1a)
+    gather_x(w2_back, w2_x, w2a)
+
+    for dz in (1, 3, 2):
+        zh_sums[dz].wait_recv()
+        final += c3r[dz - 1].astype(F32)
     prompt_out[0] = final[:PKEYS]
     prompt_out[1] = final[PKEYS : 2 * PKEYS]
     suffix_out[0] = final[2 * PKEYS :]
@@ -390,7 +423,7 @@
 def shards(prompt, suffix, queries, key_up, value_up, out_grad, fork_prompt, suffix_length):
     vmem = pl.BlockSpec(memory_space=pltpu.VMEM)
     smem = pl.BlockSpec(memory_space=pltpu.SMEM)
-    copies = 96
+    copies = 128
     outs = pl.pallas_call(
         kernel,
         out_shape=(
@@ -403,29 +436,27 @@
         in_specs=[vmem] * 6 + [smem] * 2,
         out_specs=(vmem,) * 5,
         scratch_shapes=[
-            pltpu.VMEM((Y, CORE, ZH, BLOCK, WIDTH), BF16),
-            pltpu.VMEM((Y, WIDTH, KEYS), BF16),
+            pltpu.VMEM((ZH, CORE, Y, BLOCK, WIDTH), BF16),
             pltpu.VMEM((ROWS, WIDTH), BF16),
             pltpu.VMEM((WIDTH, ROWS), BF16),
             pltpu.VMEM((ROWS, LATENT), BF16),
             pltpu.VMEM((LATENT, ROWS), BF16),
             pltpu.VMEM((ROWS, HEADS * VHEAD), BF16),
             pltpu.VMEM((HEADS * NOPE, ROWS), BF16),
-            pltpu.VMEM((Y, KEYS, ROWS), F32),
-            pltpu.VMEM((Y, KEYS, ROWS), F32),
-            pltpu.VMEM((Y, KEYS, ROWS), F32),
-            pltpu.VMEM((LATENT, ROWS), F32),
+            pltpu.VMEM((ZH, KEYS, ROWS), F32),
+            pltpu.VMEM((ZH, KEYS, ROWS), F32),
+            pltpu.VMEM((ZH, KEYS, ROWS), F32),
+            pltpu.VMEM((ZH, 1, ROWS), F32),
             pltpu.VMEM((WIDTH, ROWS), F32),
-            pltpu.VMEM((Y, KEYS, ROWS), BF16),
-            pltpu.VMEM((Y, KEYS, ROWS), BF16),
-            pltpu.VMEM((Y, CORE, ZH * BLOCK, WIDTH), F32),
+            pltpu.VMEM((WIDTH, ROWS), F32),
+            pltpu.VMEM((ZH, CORE, Y * BLOCK, WIDTH), F32),
             pltpu.VMEM((16, TILE), F32),
             pltpu.VMEM((ZL * X, 16, TILE), F32),
-            pltpu.VMEM((Y, ZH * BLOCK, WIDTH), BF16),
-            pltpu.VMEM((Y, ZH * BLOCK, WIDTH), BF16),
-            pltpu.VMEM((Y - 1, ZH * BLOCK, WIDTH), BF16),
-            pltpu.VMEM((Y - 1, ZH * BLOCK, WIDTH), BF16),
-            pltpu.VMEM((ZH, BLOCK, WIDTH), BF16),
+            pltpu.VMEM((ZH, Y * BLOCK, WIDTH), BF16),
+            pltpu.VMEM((ZH, Y * BLOCK, WIDTH), BF16),
+            pltpu.VMEM((ZH, Y, BLOCK, WIDTH), BF16),
+            pltpu.VMEM((ZH, Y - 1, BLOCK, WIDTH), BF16),
+            pltpu.VMEM((ZH - 1, BLOCK, WIDTH), BF16),
             pltpu.VMEM((ZH - 1, BLOCK, WIDTH), BF16),
             pltpu.VMEM((X, ZL, W1, TILE), F32),
             pltpu.VMEM((X, ZL, W1, TILE), BF16),

time: 106 us -> 95.9 us (0.905)
  the two profiles are of different devices: /device:TPU:1 before, /device:TPU:32 now
where the time goes in v2:
time: 95.9 us; the launch traced here: 95.7 us
  Pallas kernels  85.7 us (89%)
  local copies, waits for them, and re-layouts  9.2 us (10%)
    pallas_call x1, Pallas kernels, shards(): pl.pallas_call(kernel, out_shape=(jax.ShapeDtypeStruct((2, PKEYS, WIDTH),...  85.7 us
    unnamed x22, local copies, waits for them, and re-layouts  5.78 us
    reshape x1, local copies, waits for them, and re-layouts, shards(): query_grad.reshape(FORKS, RECOMP, HEADS, QUERY)  2.2 us

profile of v2, /device:TPU:32, one launch (start us, length us, event | category | flops | bytes accessed | tf_op | source)
XLA Modules:
  0.0 95.7 jit_solution(3434150470558330807)
XLA Ops:
  0.6 0.0 copy-start
  0.6 0.0 copy-start.3
  0.7 0.0 copy-start.4
  0.7 0.0 copy-start.5
  0.7 0.0 copy-start.6
  0.7 1.2 %reshape.31.q_ref = bf16[640,192]{1,0:T(8,128)(2,1)S(1)} reshape(bf16[32,5,4,192]{3,2,1,0:T(4,128)(2,1)} %param.10) | data formatting | bytes 491520 | tf_op jit(solution)/shard_map/reshape | solution.py:486
  1.9 0.0 copy-done
  1.9 0.0 copy-done.3
  1.9 0.0 copy-done.4
  1.9 0.0 copy-done.5
  1.9 0.0 copy-done.6
  2.0 0.0 copy-start.1
  2.0 1.0 %copy-done.1 = bf16[4,512,128]{2,1,0:T(8,128)(2,1)S(1)} copy-done((bf16[4,512,128]{2,1,0:T(8,128)(2,1)S(1)}, bf16[4,512,128]{2,1,0:T(8,128)(2,1)}, u32[]{:S(2)}) %copy-start.1) | copy-done | bytes 524312
  3.0 0.0 copy-start.2
  3.0 0.9 copy-done.2
  3.9 85.7 %latent_backward.1 = (f32[2,8,576]{2,1,0:T(8,128)S(1)}, f32[1,16,576]{2,1,0:T(8,128)S(1)}, f32[640,192]{1,0:T(8,128)}, f32[512,512]{1,0:T(8,128)}, f32[2048,128]{1,0:T(8,128)}) custom-call(bf16[2,8,576]{2,1,0:T(8,128)(2,1)S(1)} %copy-done.3, bf16[1,16,576]{2,1,0:T(8,128)(2,1)S(1)} %copy-done.4, bf16[640,192]{1,0:T(8,128)(2,1)S(1)} %reshape.31.q_ref, ...), custom_call_target="tpu_custom_call" | custom-call | flops 8000000000 | bytes 6000000 | tf_op jit(solution)/shard_map/latent_backward/pallas_call | solution.py:427
  89.6 0.0 copy-start.8
  89.6 2.2 %reshape.35 = f32[32,5,4,192]{3,2,1,0:T(4,128)} reshape(f32[640,192]{1,0:T(8,128)} %get-tuple-element.12) | data formatting | bytes 983040 | tf_op jit(solution)/shard_map/reshape | solution.py:497
  91.8 0.6 copy.17
  92.5 0.6 copy.18
  93.1 0.0 copy-done.8
  93.1 0.0 copy-start.7
  93.1 1.0 %copy.19 = f32[4,128,512]{2,1,0:T(8,128)} copy(f32[4,128,512]{2,1,0:T(8,128)S(1)} %bitcast.9) | data formatting | bytes 2097152
  94.0 0.6 copy-done.7
  94.7 1.0 %copy.20 = f32[4,512,128]{2,1,0:T(8,128)} copy(f32[4,512,128]{2,1,0:T(8,128)S(1)} %bitcast.8) | data formatting | bytes 2097152
Async XLA Ops:
  0.6 1.3 %copy-start = (bf16[4,128,512]{2,1,0:T(8,128)(2,1)S(1)}, bf16[4,128,512]{2,1,0:T(8,128)(2,1)}, u32[]{:S(2)}) copy-start(bf16[4,128,512]{2,1,0:T(8,128)(2,1)} %param.11) | copy-start | bytes 1572868
  0.6 1.3 %copy-start.3 = (bf16[2,8,576]{2,1,0:T(8,128)(2,1)S(1)}, bf16[2,8,576]{2,1,0:T(8,128)(2,1)}, u32[]{:S(2)}) copy-start(bf16[2,8,576]{2,1,0:T(8,128)(2,1)} %prompt_ref.1) | copy-start | bytes 55300
  0.7 1.3 %copy-start.4 = (bf16[1,16,576]{2,1,0:T(8,128)(2,1)S(1)}, bf16[1,16,576]{2,1,0:T(8,128)(2,1)}, u32[]{:S(2)}) copy-start(bf16[1,16,576]{2,1,0:T(8,128)(2,1)} %suffix_ref.1) | copy-start | bytes 55300
  0.7 1.3 %copy-start.5 = (s32[32]{0:T(128)S(1)}, s32[32]{0:T(128)}, u32[]{:S(2)}) copy-start(s32[32]{0:T(128)} %fork_ref.1) | copy-start | bytes 388
  0.7 1.3 %copy-start.6 = (s32[32]{0:T(128)S(1)}, s32[32]{0:T(128)}, u32[]{:S(2)}) copy-start(s32[32]{0:T(128)} %length_ref.1) | copy-start | bytes 388
  2.0 1.0 %copy-start.1 = (bf16[4,512,128]{2,1,0:T(8,128)(2,1)S(1)}, bf16[4,512,128]{2,1,0:T(8,128)(2,1)}, u32[]{:S(2)}) copy-start(bf16[4,512,128]{2,1,0:T(8,128)(2,1)} %param.12) | copy-start | bytes 1572868
  3.0 0.9 copy-start.2
  89.6 3.4 %copy-start.8 = (f32[512,512]{1,0:T(8,128)S(1)}, f32[512,512]{1,0:T(8,128)}, u32[]{:S(2)}) copy-start(f32[512,512]{1,0:T(8,128)} %get-tuple-element.13) | copy-start | bytes 3145732
  93.1 1.6 %copy-start.7 = (f32[2048,128]{1,0:T(8,128)S(1)}, f32[2048,128]{1,0:T(8,128)}, u32[]{:S(2)}) copy-start(f32[2048,128]{1,0:T(8,128)} %get-tuple-element.14) | copy-start | bytes 3145732

commit v3 on v2

--- a/solution.py
+++ b/solution.py
@@ -57,12 +57,12 @@
 
 
 def kernel(
-    prompt_ref, suffix_ref, q_ref, ku_ref, vu_ref, og_ref, fork_ref, length_ref,
-    prompt_out, suffix_out, query_out, key_up_out, value_up_out,
+    prompt_ref, suffix_ref, q_any, ku_any, vu_any, og_any, fork_ref, length_ref,
+    keys_out, w1_out, w2_out,
     keys, qry, qry_t, lgr, lgr_t, og_exp, qn_exp_t, bias, score, pgrad, peaks,
     acc_t, dif_t, kgrad, stat, stat_all, c1s, c1r, c2s, c2r, c3s, c3r,
     w1f, w1b, w1x, w1m, w1z, w1a, w2f, w2b, w2x, w2m, w2z, w2a,
-    send_sem, recv_sem,
+    q_ref, ku_ref, vu_ref, og_ref, send_sem, recv_sem, load_sem,
 ):
     ctx, sample = lax.axis_index("ctx"), lax.axis_index("sample")
     zl, x = ctx // X, ctx % X
@@ -86,6 +86,14 @@
         return (zl + d + ZL) % ZL
 
     sems = Sems(send_sem, recv_sem)
+    loads = [
+        pltpu.make_async_copy(src, dst, load_sem.at[k])
+        for k, (src, dst) in enumerate(
+            ((q_any, q_ref), (ku_any, ku_ref), (vu_any, vu_ref), (og_any, og_ref))
+        )
+    ]
+    for made in loads:
+        made.start()
 
     partners = [sibling]
     partners += [at(zh_=zh_by(d)) for d in range(1, ZH)]
@@ -127,8 +135,9 @@
 
     def project(t, carry):
         rows = pl.ds(pl.multiple_of(t * TILE, TILE), TILE)
-        q = q_ref[rows, :]
-        og = og_ref[rows, :]
+        steps = pl.ds(t * (TILE // HEADS), TILE // HEADS)
+        q = q_ref[steps].reshape(TILE, QUERY)
+        og = og_ref[steps].reshape(TILE, VHEAD)
         head = lax.broadcasted_iota(jnp.int32, (TILE, NOPE), 0) & (HEADS - 1)
         q_nope = q[:, :NOPE]
         zero = jnp.zeros_like(q_nope)
@@ -153,6 +162,8 @@
         lgr_t[:, rows] = grad.T
         return carry
 
+    for made in loads:
+        made.wait()
     lax.fori_loop(0, TILES, project, 0)
 
     def gather_rows(f, carry):
@@ -272,13 +283,15 @@
     def send_x(src, dst):
         made = {}
         for e in (2, 1, 3, 0):
+            to = zl_by(e)
             made[e] = [
-                sems.copy(
-                    src.at[x_by(d), zl_by(e)], dst.at[d - 1, zl_by(e)], at(x_=x_by(d))
-                )
+                sems.copy(src(x_by(d), to), dst.at[d - 1, to], at(x_=x_by(d)))
                 for d in (2, 1, 3)
             ]
         return made
+
+    def w2_rows(to_x, to_zl):
+        return pl.ds(pl.multiple_of((to_x * ZL + to_zl) * W2, W2), W2)
 
     scaled = (acc_t[:LATENT, :] * weight).astype(BF16)
     for h in range(HEADS):
@@ -286,28 +299,29 @@
         part = dot(scaled, og_exp[:, cols]).reshape(ZL, W1, TILE)
         w1f[h] = part
         w1b[h] = part.astype(BF16)
-    w1_x = send_x(w1b, w1x)
+    w1_x = send_x(lambda *to: w1b.at[to], w1x)
 
     shift = row_delta - mean
     factor = weight * SCALE
     lat = (factor * (dif_t[:LATENT, :] - shift * acc_t[:LATENT, :])).astype(BF16)
     rope = factor * (dif_t[LATENT:, :] - shift * acc_t[LATENT:, :])
-    kup = dot_nt(qn_exp_t[...], lat)
+
+    def put(row, part):
+        w2f[row : row + part.shape[0], :] = part
+        w2b[row : row + part.shape[0], :] = part.astype(BF16)
+
     for b in range(LATENT // TILE):
-        w2f[b * 512 : (b + 1) * 512, :] = kup[:, b * TILE : (b + 1) * TILE]
+        put(b * 512, dot_nt(qn_exp_t[...], lat[b * TILE : (b + 1) * TILE, :]))
     spread = dot(ku_ref[...], lat)
     head_of = lane & (HEADS - 1)
-    nope = jnp.zeros((NOPE, ROWS), F32)
-    for h in range(HEADS):
+    nope = spread[:NOPE, :]
+    for h in range(1, HEADS):
         nope = jnp.where(head_of == h, spread[h * NOPE : (h + 1) * NOPE, :], nope)
     for t in range(TILES):
         cols = slice(t * TILE, (t + 1) * TILE)
-        base = 2048 + t * QUERY
-        w2f[base : base + NOPE, :] = nope[:, cols]
-        w2f[base + NOPE : base + QUERY, :] = rope[:, cols]
-    w2f[2048 + TILES * QUERY : 3072, :] = jnp.zeros((64, TILE), F32)
-    w2b[...] = w2f[...].reshape(X, ZL, W2, TILE).astype(BF16)
-    w2_x = send_x(w2b, w2x)
+        put(2048 + t * QUERY, jnp.concatenate([nope[:, cols], rope[:, cols]], 0))
+    put(2048 + TILES * QUERY, jnp.zeros((64, TILE), F32))
+    w2_x = send_x(lambda *to: w2b.at[w2_rows(*to), :], w2x)
 
     core_sums, y_sums, zh_sums = {}, {}, {}
 
@@ -376,65 +390,67 @@
             back[e].wait_recv()
             out += spread_x(whole, e)
 
-    def w2_rows(to):
-        return w2f[pl.ds(pl.multiple_of((x * ZL + to) * W2, W2), W2), :]
-
-    key_grads(2)
-    key_grads(1)
-    add_cores(2)
-    key_grads(3)
-    add_cores(1)
-    key_grads(0)
+    for dz in (2, 1, 3, 0):
+        key_grads(dz)
     w1_z = sum_x(w1_x, lambda to: w1f[x, to], w1x, w1m, w1z)
-    add_cores(3)
-    add_ys(2)
-    w2_z = sum_x(w2_x, w2_rows, w2x, w2m, w2z)
-    add_ys(1)
-    add_ys(3)
-    add_cores(0)
+    for dz in (2, 1, 3, 0):
+        add_cores(dz)
     w1_back, w1_x = sum_zl(w1_z, w1m, w1z, w1a)
+    w2_z = sum_x(w2_x, lambda to: w2f[w2_rows(x, to), :], w2x, w2m, w2z)
+    for dz in (2, 1, 3):
+        add_ys(dz)
     final = add_ys(0)
+    gather_x(w1_back, w1_x, w1a)
     w2_back, w2_x = sum_zl(w2_z, w2m, w2z, w2a)
-    gather_x(w1_back, w1_x, w1a)
     gather_x(w2_back, w2_x, w2a)
 
     for dz in (1, 3, 2):
         zh_sums[dz].wait_recv()
         final += c3r[dz - 1].astype(F32)
-    prompt_out[0] = final[:PKEYS]
-    prompt_out[1] = final[PKEYS : 2 * PKEYS]
-    suffix_out[0] = final[2 * PKEYS :]
-
+    keys_out[...] = final
     for made in w1_x:
         made.wait_recv()
-    value_up_out[...] = w1a[...].reshape(HEADS * LATENT, VHEAD).astype(F32)
+    w1_out[...] = w1a[...].reshape(HEADS * LATENT, VHEAD)
     for made in w2_x:
         made.wait_recv()
-    w2f[...] = w2a[...].reshape(3072, TILE).astype(F32)
+    w2_out[...] = w2a[...].reshape(X * ZL * W2, TILE)
+    for made in sems.started:
+        made.wait_send()
+
+
+def unpack(keys_ref, w1_ref, w2_ref, prompt_out, suffix_out, query_out, key_up_out, value_up_out):
+    prompt_out[0] = keys_ref[:PKEYS, :]
+    prompt_out[1] = keys_ref[PKEYS : 2 * PKEYS, :]
+    suffix_out[0] = keys_ref[2 * PKEYS :, :]
+    value_up_out[...] = w1_ref[...].astype(F32)
     for b in range(LATENT // TILE):
-        key_up_out[:, b * TILE : (b + 1) * TILE] = w2f[b * 512 : (b + 1) * 512, :]
+        key_up_out[:, b * TILE : (b + 1) * TILE] = w2_ref[b * 512 : (b + 1) * 512, :].astype(F32)
+    steps = TILE // HEADS
     for t in range(TILES):
         base = 2048 + t * QUERY
-        query_out[t * TILE : (t + 1) * TILE, :] = w2f[base : base + QUERY, :].T
-    for made in sems.started:
-        made.wait_send()
+        part = w2_ref[base : base + QUERY, :].astype(F32).T
+        query_out[t * steps : (t + 1) * steps] = part.reshape(steps, HEADS, QUERY)
 
 
 def shards(prompt, suffix, queries, key_up, value_up, out_grad, fork_prompt, suffix_length):
     vmem = pl.BlockSpec(memory_space=pltpu.VMEM)
     smem = pl.BlockSpec(memory_space=pltpu.SMEM)
     copies = 128
-    outs = pl.pallas_call(
+    hbm = pl.BlockSpec(memory_space=pltpu.HBM)
+
+    def in_hbm(v):
+        return pltpu.with_memory_space_constraint(v, pltpu.HBM)
+
+    steps = FORKS * RECOMP
+    sums = pl.pallas_call(
         kernel,
         out_shape=(
-            jax.ShapeDtypeStruct((2, PKEYS, WIDTH), F32),
-            jax.ShapeDtypeStruct((1, SKEYS, WIDTH), F32),
-            jax.ShapeDtypeStruct((ROWS, QUERY), F32),
-            jax.ShapeDtypeStruct((HEADS * NOPE, LATENT), F32),
-            jax.ShapeDtypeStruct((HEADS * LATENT, VHEAD), F32),
+            jax.ShapeDtypeStruct((BLOCK, WIDTH), F32),
+            jax.ShapeDtypeStruct((HEADS * LATENT, VHEAD), BF16),
+            jax.ShapeDtypeStruct((X * ZL * W2, TILE), BF16),
         ),
-        in_specs=[vmem] * 6 + [smem] * 2,
-        out_specs=(vmem,) * 5,
+        in_specs=[vmem] * 2 + [hbm] * 4 + [smem] * 2,
+        out_specs=(vmem,) * 3,
         scratch_shapes=[
             pltpu.VMEM((ZH, CORE, Y, BLOCK, WIDTH), BF16),
             pltpu.VMEM((ROWS, WIDTH), BF16),
@@ -465,16 +481,21 @@
             pltpu.VMEM((ZL - 1, W1, TILE), BF16),
             pltpu.VMEM((X, ZL, W1, TILE), BF16),
             pltpu.VMEM((X * ZL * W2, TILE), F32),
-            pltpu.VMEM((X, ZL, W2, TILE), BF16),
+            pltpu.VMEM((X * ZL * W2, TILE), BF16),
             pltpu.VMEM((X - 1, ZL, W2, TILE), BF16),
             pltpu.VMEM((ZL, W2, TILE), BF16),
             pltpu.VMEM((ZL - 1, W2, TILE), BF16),
             pltpu.VMEM((X, ZL, W2, TILE), BF16),
+            pltpu.VMEM((steps, HEADS, QUERY), BF16),
+            pltpu.VMEM((HEADS * NOPE, LATENT), BF16),
+            pltpu.VMEM((HEADS * LATENT, VHEAD), BF16),
+            pltpu.VMEM((steps, HEADS, VHEAD), BF16),
             pltpu.SemaphoreType.DMA((copies,)),
             pltpu.SemaphoreType.DMA((copies,)),
+            pltpu.SemaphoreType.DMA((4,)),
         ],
         compiler_params=pltpu.CompilerParams(
-            collective_id=0, has_side_effects=True, vmem_limit_bytes=52 << 20
+            collective_id=0, has_side_effects=True, vmem_limit_bytes=42 << 20
         ),
         cost_estimate=pl.CostEstimate(
             flops=8_000_000_000, bytes_accessed=6_000_000, transcendentals=700_000
@@ -483,14 +504,27 @@
     )(
         prompt,
         suffix,
-        queries.reshape(ROWS, QUERY),
-        key_up.reshape(HEADS * NOPE, LATENT),
-        value_up.reshape(HEADS * LATENT, VHEAD),
-        out_grad.reshape(ROWS, VHEAD),
+        in_hbm(queries.reshape(steps, HEADS, QUERY)),
+        in_hbm(key_up.reshape(HEADS * NOPE, LATENT)),
+        in_hbm(value_up.reshape(HEADS * LATENT, VHEAD)),
+        in_hbm(out_grad.reshape(steps, HEADS, VHEAD)),
         fork_prompt,
         suffix_length,
     )
-    prompt_grad, suffix_grad, query_grad, key_up_grad, value_up_grad = outs
+    prompt_grad, suffix_grad, query_grad, key_up_grad, value_up_grad = pl.pallas_call(
+        unpack,
+        out_shape=(
+            jax.ShapeDtypeStruct((2, PKEYS, WIDTH), F32),
+            jax.ShapeDtypeStruct((1, SKEYS, WIDTH), F32),
+            jax.ShapeDtypeStruct((steps, HEADS, QUERY), F32),
+            jax.ShapeDtypeStruct((HEADS * NOPE, LATENT), F32),
+            jax.ShapeDtypeStruct((HEADS * LATENT, VHEAD), F32),
+        ),
+        in_specs=[vmem] * 3,
+        out_specs=(vmem,) * 5,
+        compiler_params=pltpu.CompilerParams(vmem_limit_bytes=16 << 20),
+        name="unpack_grads",
+    )(*sums)
     return (
         prompt_grad,
         suffix_grad,

time: 95.9 us -> 86.6 us (0.903)
  the two profiles are of different devices: /device:TPU:32 before, /device:TPU:64 now
where the time goes in v3:
time: 86.6 us; the launch traced here: 86.3 us
  Pallas kernels  83.5 us (96%)
  local copies, waits for them, and re-layouts  2.11 us (2%)
    pallas_call x1, Pallas kernels, shards(): pl.pallas_call(kernel, out_shape=(jax.ShapeDtypeStruct((BLOCK, WIDTH), F3...  81.7 us
    unnamed x8, local copies, waits for them, and re-layouts  2.11 us
    pallas_call x1, Pallas kernels, shards(): pl.pallas_call(unpack, out_shape=(jax.ShapeDtypeStruct((2, PKEYS, WIDTH),...  1.8 us

profile of v3, /device:TPU:64, one launch (start us, length us, event | category | flops | bytes accessed | tf_op | source)
XLA Modules:
  0.0 86.3 jit_solution(14425106318738549607)
XLA Ops:
  0.6 0.0 copy-start.2
  0.6 0.0 copy-start.3
  0.7 0.6 copy-done.2
  1.3 0.0 copy-done.3
  1.3 0.0 copy-start
  1.3 0.7 copy-done
  2.0 0.0 copy-start.1
  2.0 0.7 copy-done.1
  2.8 81.7 %latent_backward.1 = (f32[32,576]{1,0:T(8,128)S(1)}, bf16[2048,128]{1,0:T(8,128)(2,1)S(1)}, bf16[3072,128]{1,0:T(8,128)(2,1)S(1)}) custom-call(bf16[2,8,576]{2,1,0:T(8,128)(2,1)S(1)} %copy-done, bf16[1,16,576]{2,1,0:T(8,128)(2,1)S(1)} %copy-done.1, bf16[160,4,192]{2,1,0:T(4,128)(2,1)} %bitcast.12, bf16[512,512]{1,0:T(8,128)(2,1)} %bitcast.10, ...), custom_call_target="tpu_custom_call" | custom-call | flops 8000000000 | bytes 6000000 | tf_op jit(solution)/shard_map/latent_backward/pallas_call | solution.py:445
  84.5 1.8 %unpack_grads.1 = (f32[2,8,576]{2,1,0:T(8,128)}, f32[1,16,576]{2,1,0:T(8,128)}, f32[160,4,192]{2,1,0:T(4,128)}, f32[512,512]{1,0:T(8,128)}, f32[2048,128]{1,0:T(8,128)}) custom-call(f32[32,576]{1,0:T(8,128)S(1)} %get-tuple-element.13.keys_ref, bf16[2048,128]{1,0:T(8,128)(2,1)S(1)} %get-tuple-element.14.w1_ref, bf16[3072,128]{1,0:T(8,128)(2,1)S(1)} %get-tuple-element.15.w2_ref), custom_call_target="tpu_custom_call" | custom-call | tf_op jit(solution)/shard_map/unpack_grads/pallas_call | solution.py:514
Async XLA Ops:
  0.6 0.7 copy-start.2
  0.6 0.7 copy-start.3
  1.3 0.7 copy-start
  2.0 0.7 copy-start.1

commit v4 on v3

--- a/solution.py
+++ b/solution.py
@@ -24,8 +24,9 @@
 BLOCK = 2 * PKEYS + SKEYS
 KEYS = CORE * Y * BLOCK
 SCALE = QUERY**-0.5
-W1 = HEADS * LATENT // 16
-W2 = 192
+W1 = HEADS * LATENT
+W2 = HEADS * NOPE * LATENT // TILE
+W3 = 1024
 
 
 def dot(a, b):
@@ -58,10 +59,10 @@
 
 def kernel(
     prompt_ref, suffix_ref, q_any, ku_any, vu_any, og_any, fork_ref, length_ref,
-    keys_out, w1_out, w2_out,
+    keys_out, w1_out, w2_out, w3_out,
     keys, qry, qry_t, lgr, lgr_t, og_exp, qn_exp_t, bias, score, pgrad, peaks,
-    acc_t, dif_t, kgrad, stat, stat_all, c1s, c1r, c2s, c2r, c3s, c3r,
-    w1f, w1b, w1x, w1m, w1z, w1a, w2f, w2b, w2x, w2m, w2z, w2a,
+    acc_t, dif_t, kgrad, stat, stat_all, c1s, c1r, c2s, c2r, c3s, c3h, c3r,
+    w1f, w1b, w1x, w1m, w1z, w1a, w2f, w2b, w2x, w2m, w2z, w2a, w3f, w3b, w3x, w3m, w3z, w3a,
     q_ref, ku_ref, vu_ref, og_ref, send_sem, recv_sem, load_sem,
 ):
     ctx, sample = lax.axis_index("ctx"), lax.axis_index("sample")
@@ -96,7 +97,7 @@
         made.start()
 
     partners = [sibling]
-    partners += [at(zh_=zh_by(d)) for d in range(1, ZH)]
+    partners += [at(zh_=zh_by(d)) for d in (1, -1)]
     partners += [at(y_=y_by(d)) for d in range(1, Y)]
     partners += [at(zl_=zl_by(a), x_=x_by(b)) for a in range(ZL) for b in range(X) if a + b]
     barrier = pltpu.get_barrier_semaphore()
@@ -111,13 +112,20 @@
     from_zh = {}
     from_y = {}
     from_core = {}
-    for d in (2, 1, 3):
+    for d in (1, 3):
         block = keys.at[zh, core, y]
-        from_zh[d] = sems.copy(block, block, at(zh_=zh_by(d)))
+        from_zh[d] = [sems.copy(block, block, at(zh_=zh_by(d)))]
+    half = BLOCK // 2
+
+    def relay(d, rows):
+        from_zh[d][0].wait_recv()
+        part = keys.at[zh_by(-d), core, y, rows]
+        from_zh.setdefault(2, []).append(sems.copy(part, part, at(zh_=zh_by(d))))
 
     def spread_y(dz):
-        if dz:
-            from_zh[dz].wait_recv()
+        if dz == 2:
+            for made in from_zh[dz]:
+                made.wait_recv()
         block = keys.at[zh_by(-dz), core, y]
         from_y[dz] = [sems.copy(block, block, at(y_=y_by(d))) for d in (2, 1, 3)]
 
@@ -164,7 +172,12 @@
 
     for made in loads:
         made.wait()
-    lax.fori_loop(0, TILES, project, 0)
+    lax.fori_loop(0, 2, project, 0)
+    relay(1, pl.ds(0, half))
+    relay(3, pl.ds(half, half))
+    spread_y(1)
+    spread_y(3)
+    lax.fori_loop(2, TILES, project, 0)
 
     def gather_rows(f, carry):
         limit, prompt = carry
@@ -233,8 +246,6 @@
         return both
 
     part, *state = scores_of(0)
-    spread_y(1)
-    spread_y(3)
     acc_t[...], dif_t[...] = sums_of(part, state[2])
     to_core(1)
     to_core(3)
@@ -280,38 +291,91 @@
     top, inverse, row_delta = as_row(top), as_row(inverse), as_row(whole_delta * inverse)
     weight = jnp.exp((peak - top) * SCALE) * inverse
 
-    def send_x(src, dst):
-        made = {}
-        for e in (2, 1, 3, 0):
-            to = zl_by(e)
-            made[e] = [
-                sems.copy(src(x_by(d), to), dst.at[d - 1, to], at(x_=x_by(d)))
-                for d in (2, 1, 3)
-            ]
-        return made
-
-    def w2_rows(to_x, to_zl):
-        return pl.ds(pl.multiple_of((to_x * ZL + to_zl) * W2, W2), W2)
-
+    class Part:
+        def __init__(self, full, sent, from_x, middle, from_zl, whole):
+            self.full, self.sent, self.from_x = full, sent, from_x
+            self.middle, self.from_zl, self.whole = middle, from_zl, whole
+            self.rows = full.shape[0] // (X * ZL)
+
+        def block(self, to_x, to_zl):
+            return pl.ds(pl.multiple_of((to_x * ZL + to_zl) * self.rows, self.rows), self.rows)
+
+        def put(self, row, part):
+            self.full[row : row + part.shape[0], :] = part
+            self.sent[row : row + part.shape[0], :] = part.astype(BF16)
+
+        def send_x(self):
+            self.at_x = {}
+            for e in (2, 1, 3, 0):
+                to = zl_by(e)
+                self.at_x[e] = [
+                    sems.copy(
+                        self.sent.at[self.block(x_by(d), to), :],
+                        self.from_x.at[d - 1, to],
+                        at(x_=x_by(d)),
+                    )
+                    for d in (2, 1, 3)
+                ]
+
+        def sum_x(self):
+            self.at_zl = []
+            for e in (2, 1, 3, 0):
+                for made in self.at_x[e]:
+                    made.wait_recv()
+                to = zl_by(e)
+                add = self.full[self.block(x, to), :]
+                for i in range(X - 1):
+                    add += self.from_x[i, to].astype(F32)
+                self.middle[to] = add.astype(BF16)
+                if e:
+                    self.at_zl.append(
+                        sems.copy(self.middle.at[to], self.from_zl.at[e - 1], at(zl_=to))
+                    )
+
+        def spread_x(self, e):
+            block = self.whole.at[self.block(x, zl_by(-e)), :]
+            return [sems.copy(block, block, at(x_=x_by(d))) for d in (2, 1, 3)]
+
+        def sum_zl(self):
+            for made in self.at_zl:
+                made.wait_recv()
+            add = self.middle[zl].astype(F32)
+            for i in range(ZL - 1):
+                add += self.from_zl[i].astype(F32)
+            own = self.block(x, zl)
+            self.whole[own, :] = add.astype(BF16)
+            block = self.whole.at[own, :]
+            self.back = {e: sems.copy(block, block, at(zl_=zl_by(e))) for e in (2, 1, 3)}
+            self.out = self.spread_x(0)
+
+        def gather_x(self):
+            for e in (1, 3, 2):
+                self.back[e].wait_recv()
+                self.out += self.spread_x(e)
+
+        def done(self, result):
+            for made in self.out:
+                made.wait_recv()
+            result[...] = self.whole[...]
+
+    value_part = Part(w1f, w1b, w1x, w1m, w1z, w1a)
+    key_part = Part(w2f, w2b, w2x, w2m, w2z, w2a)
+    query_part = Part(w3f, w3b, w3x, w3m, w3z, w3a)
     scaled = (acc_t[:LATENT, :] * weight).astype(BF16)
     for h in range(HEADS):
         cols = slice(h * VHEAD, (h + 1) * VHEAD)
-        part = dot(scaled, og_exp[:, cols]).reshape(ZL, W1, TILE)
-        w1f[h] = part
-        w1b[h] = part.astype(BF16)
-    w1_x = send_x(lambda *to: w1b.at[to], w1x)
+        value_part.put(h * LATENT, dot(scaled, og_exp[:, cols]))
+    value_part.send_x()
 
     shift = row_delta - mean
     factor = weight * SCALE
     lat = (factor * (dif_t[:LATENT, :] - shift * acc_t[:LATENT, :])).astype(BF16)
     rope = factor * (dif_t[LATENT:, :] - shift * acc_t[LATENT:, :])
-
-    def put(row, part):
-        w2f[row : row + part.shape[0], :] = part
-        w2b[row : row + part.shape[0], :] = part.astype(BF16)
-
     for b in range(LATENT // TILE):
-        put(b * 512, dot_nt(qn_exp_t[...], lat[b * TILE : (b + 1) * TILE, :]))
+        key_part.put(
+            b * HEADS * NOPE, dot_nt(qn_exp_t[...], lat[b * TILE : (b + 1) * TILE, :])
+        )
+    key_part.send_x()
     spread = dot(ku_ref[...], lat)
     head_of = lane & (HEADS - 1)
     nope = spread[:NOPE, :]
@@ -319,9 +383,9 @@
         nope = jnp.where(head_of == h, spread[h * NOPE : (h + 1) * NOPE, :], nope)
     for t in range(TILES):
         cols = slice(t * TILE, (t + 1) * TILE)
-        put(2048 + t * QUERY, jnp.concatenate([nope[:, cols], rope[:, cols]], 0))
-    put(2048 + TILES * QUERY, jnp.zeros((64, TILE), F32))
-    w2_x = send_x(lambda *to: w2b.at[w2_rows(*to), :], w2x)
+        query_part.put(t * QUERY, jnp.concatenate([nope[:, cols], rope[:, cols]], 0))
+    query_part.put(TILES * QUERY, jnp.zeros((W3 - TILES * QUERY, TILE), F32))
+    query_part.send_x()
 
     core_sums, y_sums, zh_sums = {}, {}, {}
 
@@ -353,72 +417,58 @@
         mine = kgrad[zh_by(-dz), core, rows, :]
         for i in range(Y - 1):
             mine += c2r[dz, i].astype(F32)
-        if dz == 0:
-            return mine
-        c3s[dz - 1] = mine.astype(BF16)
-        zh_sums[dz] = sems.copy(c3s.at[dz - 1], c3r.at[dz - 1], at(zh_=zh_by(-dz)))
-
-    def sum_x(made, full, came, middle, dst):
-        out = []
-        for e in (2, 1, 3, 0):
-            for m in made[e]:
-                m.wait_recv()
-            to = zl_by(e)
-            add = full(to) + came[0, to].astype(F32) + came[1, to].astype(F32)
-            middle[to] = (add + came[2, to].astype(F32)).astype(BF16)
-            if e:
-                out.append(sems.copy(middle.at[to], dst.at[e - 1], at(zl_=to)))
-        return out
-
-    def spread_x(whole, e):
-        block = whole.at[x, zl_by(-e)]
-        return [sems.copy(block, block, at(x_=x_by(d))) for d in (2, 1, 3)]
-
-    def sum_zl(made, middle, came, whole):
-        for m in made:
-            m.wait_recv()
-        add = middle[zl].astype(F32)
-        for i in range(ZL - 1):
-            add += came[i].astype(F32)
-        whole[x, zl] = add.astype(BF16)
-        block = whole.at[x, zl]
-        back = {e: sems.copy(block, block, at(zl_=zl_by(e))) for e in (2, 1, 3)}
-        return back, spread_x(whole, 0)
-
-    def gather_x(back, out, whole):
-        for e in (1, 3, 2):
-            back[e].wait_recv()
-            out += spread_x(whole, e)
+        return mine
+
+    def send_far(mine):
+        c3s[2] = mine.astype(BF16)
+        return [
+            sems.copy(c3s.at[2, pl.ds(0, half)], c3h.at[0], at(zh_=zh_by(1))),
+            sems.copy(c3s.at[2, pl.ds(half, half)], c3h.at[1], at(zh_=zh_by(-1))),
+        ]
+
+    def send_near(halves, up, down):
+        for made in halves:
+            made.wait_recv()
+        c3s[0, :half] = (up[:half] + c3h[0].astype(F32)).astype(BF16)
+        c3s[0, half:] = up[half:].astype(BF16)
+        c3s[1, :half] = down[:half].astype(BF16)
+        c3s[1, half:] = (down[half:] + c3h[1].astype(F32)).astype(BF16)
+        return [
+            sems.copy(c3s.at[0], c3r.at[0], at(zh_=zh_by(1))),
+            sems.copy(c3s.at[1], c3r.at[1], at(zh_=zh_by(-1))),
+        ]
 
     for dz in (2, 1, 3, 0):
         key_grads(dz)
-    w1_z = sum_x(w1_x, lambda to: w1f[x, to], w1x, w1m, w1z)
+    value_part.sum_x()
     for dz in (2, 1, 3, 0):
         add_cores(dz)
-    w1_back, w1_x = sum_zl(w1_z, w1m, w1z, w1a)
-    w2_z = sum_x(w2_x, lambda to: w2f[w2_rows(x, to), :], w2x, w2m, w2z)
-    for dz in (2, 1, 3):
-        add_ys(dz)
-    final = add_ys(0)
-    gather_x(w1_back, w1_x, w1a)
-    w2_back, w2_x = sum_zl(w2_z, w2m, w2z, w2a)
-    gather_x(w2_back, w2_x, w2a)
-
-    for dz in (1, 3, 2):
-        zh_sums[dz].wait_recv()
-        final += c3r[dz - 1].astype(F32)
-    keys_out[...] = final
-    for made in w1_x:
+    key_part.sum_x()
+    query_part.sum_x()
+    halves = send_far(add_ys(2))
+    value_part.sum_zl()
+    up, down, final = add_ys(3), add_ys(1), add_ys(0)
+    key_part.sum_zl()
+    value_part.gather_x()
+    query_part.sum_zl()
+    near = send_near(halves, up, down)
+    key_part.gather_x()
+    query_part.gather_x()
+
+    for made in near:
         made.wait_recv()
-    w1_out[...] = w1a[...].reshape(HEADS * LATENT, VHEAD)
-    for made in w2_x:
-        made.wait_recv()
-    w2_out[...] = w2a[...].reshape(X * ZL * W2, TILE)
+    keys_out[...] = final + c3r[0].astype(F32) + c3r[1].astype(F32)
+    value_part.done(w1_out)
+    key_part.done(w2_out)
+    query_part.done(w3_out)
     for made in sems.started:
         made.wait_send()
 
 
-def unpack(keys_ref, w1_ref, w2_ref, prompt_out, suffix_out, query_out, key_up_out, value_up_out):
+def unpack(
+    keys_ref, w1_ref, w2_ref, w3_ref,
+    prompt_out, suffix_out, query_out, key_up_out, value_up_out,
+):
     prompt_out[0] = keys_ref[:PKEYS, :]
     prompt_out[1] = keys_ref[PKEYS : 2 * PKEYS, :]
     suffix_out[0] = keys_ref[2 * PKEYS :, :]
@@ -427,15 +477,26 @@
         key_up_out[:, b * TILE : (b + 1) * TILE] = w2_ref[b * 512 : (b + 1) * 512, :].astype(F32)
     steps = TILE // HEADS
     for t in range(TILES):
-        base = 2048 + t * QUERY
-        part = w2_ref[base : base + QUERY, :].astype(F32).T
+        part = w3_ref[t * QUERY : (t + 1) * QUERY, :].astype(F32).T
         query_out[t * steps : (t + 1) * steps] = part.reshape(steps, HEADS, QUERY)
+
+
+def part_scratch(rows):
+    block = rows // (X * ZL)
+    return (
+        pltpu.VMEM((rows, TILE), F32),
+        pltpu.VMEM((rows, TILE), BF16),
+        pltpu.VMEM((X - 1, ZL, block, TILE), BF16),
+        pltpu.VMEM((ZL, block, TILE), BF16),
+        pltpu.VMEM((ZL - 1, block, TILE), BF16),
+        pltpu.VMEM((rows, TILE), BF16),
+    )
 
 
 def shards(prompt, suffix, queries, key_up, value_up, out_grad, fork_prompt, suffix_length):
     vmem = pl.BlockSpec(memory_space=pltpu.VMEM)
     smem = pl.BlockSpec(memory_space=pltpu.SMEM)
-    copies = 128
+    copies = 152
     hbm = pl.BlockSpec(memory_space=pltpu.HBM)
 
     def in_hbm(v):
@@ -446,11 +507,12 @@
         kernel,
         out_shape=(
             jax.ShapeDtypeStruct((BLOCK, WIDTH), F32),
-            jax.ShapeDtypeStruct((HEADS * LATENT, VHEAD), BF16),
-            jax.ShapeDtypeStruct((X * ZL * W2, TILE), BF16),
+            jax.ShapeDtypeStruct((W1, TILE), BF16),
+            jax.ShapeDtypeStruct((W2, TILE), BF16),
+            jax.ShapeDtypeStruct((W3, TILE), BF16),
         ),
         in_specs=[vmem] * 2 + [hbm] * 4 + [smem] * 2,
-        out_specs=(vmem,) * 3,
+        out_specs=(vmem,) * 4,
         scratch_shapes=[
             pltpu.VMEM((ZH, CORE, Y, BLOCK, WIDTH), BF16),
             pltpu.VMEM((ROWS, WIDTH), BF16),
@@ -473,19 +535,11 @@
             pltpu.VMEM((ZH, Y, BLOCK, WIDTH), BF16),
             pltpu.VMEM((ZH, Y - 1, BLOCK, WIDTH), BF16),
             pltpu.VMEM((ZH - 1, BLOCK, WIDTH), BF16),
-            pltpu.VMEM((ZH - 1, BLOCK, WIDTH), BF16),
-            pltpu.VMEM((X, ZL, W1, TILE), F32),
-            pltpu.VMEM((X, ZL, W1, TILE), BF16),
-            pltpu.VMEM((X - 1, ZL, W1, TILE), BF16),
-            pltpu.VMEM((ZL, W1, TILE), BF16),
-            pltpu.VMEM((ZL - 1, W1, TILE), BF16),
-            pltpu.VMEM((X, ZL, W1, TILE), BF16),
-            pltpu.VMEM((X * ZL * W2, TILE), F32),
-            pltpu.VMEM((X * ZL * W2, TILE), BF16),
-            pltpu.VMEM((X - 1, ZL, W2, TILE), BF16),
-            pltpu.VMEM((ZL, W2, TILE), BF16),
-            pltpu.VMEM((ZL - 1, W2, TILE), BF16),
-            pltpu.VMEM((X, ZL, W2, TILE), BF16),
+            pltpu.VMEM((2, BLOCK // 2, WIDTH), BF16),
+            pltpu.VMEM((2, BLOCK, WIDTH), BF16),
+            *part_scratch(W1),
+            *part_scratch(W2),
+            *part_scratch(W3),
             pltpu.VMEM((steps, HEADS, QUERY), BF16),
             pltpu.VMEM((HEADS * NOPE, LATENT), BF16),
             pltpu.VMEM((HEADS * LATENT, VHEAD), BF16),
@@ -502,14 +556,14 @@
         ),
         name="latent_backward",
     )(
-        prompt,
-        suffix,
+        in_hbm(prompt),
+        in_hbm(suffix),
         in_hbm(queries.reshape(steps, HEADS, QUERY)),
         in_hbm(key_up.reshape(HEADS * NOPE, LATENT)),
         in_hbm(value_up.reshape(HEADS * LATENT, VHEAD)),
         in_hbm(out_grad.reshape(steps, HEADS, VHEAD)),
-        fork_prompt,
-        suffix_length,
+        in_hbm(fork_prompt),
+        in_hbm(suffix_length),
     )
     prompt_grad, suffix_grad, query_grad, key_up_grad, value_up_grad = pl.pallas_call(
         unpack,
@@ -520,7 +574,7 @@
             jax.ShapeDtypeStruct((HEADS * NOPE, LATENT), F32),
             jax.ShapeDtypeStruct((HEADS * LATENT, VHEAD), F32),
         ),
-        in_specs=[vmem] * 3,
+        in_specs=[vmem] * 4,
         out_specs=(vmem,) * 5,
         compiler_params=pltpu.CompilerParams(vmem_limit_bytes=16 << 20),
         name="unpack_grads",

time: 86.6 us -> 80 us (0.924)
  Pallas kernels: 83.5 us -> 79.2 us
  local copies, waits for them, and re-layouts: 2.11 us -> 0 us
    pallas_call x1, Pallas kernels: 81.7 us -> 77.4 us  [shards(): pl.pallas_call(kernel, out_shape=(jax.ShapeDtypeStruct((BLOCK, WIDTH), F3...]
    unnamed x8 -> x0, local copies, waits for them, and re-layouts: 2.11 us -> none
where the time goes in v4:
time: 80 us; the launch traced here: 79.9 us
  Pallas kernels  79.2 us (99%)
    pallas_call x1, Pallas kernels, shards(): pl.pallas_call(kernel, out_shape=(jax.ShapeDtypeStruct((BLOCK, WIDTH), F3...  77.4 us
    pallas_call x1, Pallas kernels, shards(): pl.pallas_call(unpack, out_shape=(jax.ShapeDtypeStruct((2, PKEYS, WIDTH),...  1.79 us

profile of v4, /device:TPU:64, one launch (start us, length us, event | category | flops | bytes accessed | tf_op | source)
XLA Modules:
  0.0 79.9 jit_solution(15963845019667087343)
XLA Ops:
  0.6 77.4 %latent_backward.1 = (f32[32,576]{1,0:T(8,128)S(1)}, bf16[2048,128]{1,0:T(8,128)(2,1)S(1)}, bf16[2048,128]{1,0:T(8,128)(2,1)S(1)}, bf16[1024,128]{1,0:T(8,128)(2,1)S(1)}) custom-call(bf16[2,8,576]{2,1,0:T(8,128)(2,1)} %prompt_ref.1, bf16[1,16,576]{2,1,0:T(8,128)(2,1)} %suffix_ref.1, bf16[160,4,192]{2,1,0:T(4,128)(2,1)} %bitcast.12, ...), custom_call_target="tpu_custom_call" | custom-call | flops 8000000000 | bytes 6000000 | tf_op jit(solution)/shard_map/latent_backward/pallas_call | solution.py:506
  78.1 1.8 %unpack_grads.1 = (f32[2,8,576]{2,1,0:T(8,128)}, f32[1,16,576]{2,1,0:T(8,128)}, f32[160,4,192]{2,1,0:T(4,128)}, f32[512,512]{1,0:T(8,128)}, f32[2048,128]{1,0:T(8,128)}) custom-call(f32[32,576]{1,0:T(8,128)S(1)} %get-tuple-element.14.keys_ref, bf16[2048,128]{1,0:T(8,128)(2,1)S(1)} %get-tuple-element.15.w1_ref, ...), custom_call_target="tpu_custom_call" | custom-call | tf_op jit(solution)/shard_map/unpack_grads/pallas_call | solution.py:568

commit v5 on v4

--- a/solution.py
+++ b/solution.py
@@ -24,9 +24,8 @@
 BLOCK = 2 * PKEYS + SKEYS
 KEYS = CORE * Y * BLOCK
 SCALE = QUERY**-0.5
-W1 = HEADS * LATENT
-W2 = HEADS * NOPE * LATENT // TILE
-W3 = 1024
+COLS = LATENT // (X * ZL)
+RCOLS = ROPE // X
 
 
 def dot(a, b):
@@ -59,10 +58,10 @@
 
 def kernel(
     prompt_ref, suffix_ref, q_any, ku_any, vu_any, og_any, fork_ref, length_ref,
-    keys_out, w1_out, w2_out, w3_out,
+    keys_out, value_out, key_up_out, query_out,
     keys, qry, qry_t, lgr, lgr_t, og_exp, qn_exp_t, bias, score, pgrad, peaks,
     acc_t, dif_t, kgrad, stat, stat_all, c1s, c1r, c2s, c2r, c3s, c3h, c3r,
-    w1f, w1b, w1x, w1m, w1z, w1a, w2f, w2b, w2x, w2m, w2z, w2a, w3f, w3b, w3x, w3m, w3z, w3a,
+    lat_s, lat_r, lat_m, lat_z, rope_s, rope_r, rope_z, abs_a, value_a, rope_a,
     q_ref, ku_ref, vu_ref, og_ref, send_sem, recv_sem, load_sem,
 ):
     ctx, sample = lax.axis_index("ctx"), lax.axis_index("sample")
@@ -99,6 +98,7 @@
     partners = [sibling]
     partners += [at(zh_=zh_by(d)) for d in (1, -1)]
     partners += [at(y_=y_by(d)) for d in range(1, Y)]
+    partners += [at(y_=y_by(d), core_=1 - core) for d in range(1, Y)]
     partners += [at(zl_=zl_by(a), x_=x_by(b)) for a in range(ZL) for b in range(X) if a + b]
     barrier = pltpu.get_barrier_semaphore()
     for device in partners:
@@ -128,12 +128,16 @@
                 made.wait_recv()
         block = keys.at[zh_by(-dz), core, y]
         from_y[dz] = [sems.copy(block, block, at(y_=y_by(d))) for d in (2, 1, 3)]
+        if dz == 2:
+            from_core[dz] = [
+                sems.copy(block, block, at(y_=y_by(d), core_=1 - core)) for d in (2, 1, 3, 0)
+            ]
 
     def to_core(dz):
         for made in from_y[dz]:
             made.wait_recv()
         part = keys.at[zh_by(-dz), core]
-        from_core[dz] = sems.copy(part, part, sibling)
+        from_core[dz] = [sems.copy(part, part, sibling)]
 
     spread_y(0)
 
@@ -205,7 +209,8 @@
     lax.fori_loop(0, Y * CORE * ZH, make_bias, 0)
 
     def scores_of(dz):
-        from_core[dz].wait_recv()
+        for made in from_core[dz]:
+            made.wait_recv()
         part = zh_by(-dz)
         tile = keys[part].reshape(KEYS, WIDTH)
         s = dot(tile, qry_t[...]) + bias[part]
@@ -252,9 +257,10 @@
     spread_y(2)
     part, *new = scores_of(1)
     state = add_sums(state, new, part)
-    to_core(2)
     part, *new = scores_of(3)
     state = add_sums(state, new, part)
+    for made in from_y[2]:
+        made.wait_recv()
     part, *new = scores_of(2)
     (peak, total, mean), _, _ = merged(state, new)
 
@@ -275,6 +281,24 @@
     stat_all[ctx] = stat[...]
 
     add_sums(state, new, part)
+    for b in range(X):
+        for c in range(ZL):
+            rows = slice((b * ZL + c) * COLS, (b * ZL + c + 1) * COLS)
+            lat_s[b, c, 0] = acc_t[rows, :].astype(BF16)
+            lat_s[b, c, 1] = dif_t[rows, :].astype(BF16)
+        rows = slice(LATENT + b * RCOLS, LATENT + (b + 1) * RCOLS)
+        rope_s[b, 0] = acc_t[rows, :].astype(BF16)
+        rope_s[b, 1] = dif_t[rows, :].astype(BF16)
+    lat_x = {}
+    for e in (2, 1, 3, 0):
+        to = zl_by(e)
+        lat_x[e] = [
+            sems.copy(lat_s.at[x_by(d), to], lat_r.at[d - 1, to], at(x_=x_by(d)))
+            for d in (2, 1, 3)
+        ]
+    rope_x = [
+        sems.copy(rope_s.at[x_by(d)], rope_r.at[d - 1], at(x_=x_by(d))) for d in (2, 1, 3)
+    ]
 
     for made in stat_copies:
         made.wait_recv()
@@ -288,104 +312,115 @@
     def as_row(v):
         return jnp.concatenate([v[t : t + 1, :] for t in range(TILES)], 1)
 
+    def weigh(d):
+        if d == 0:
+            one = stat
+        else:
+            one = stat_all.at[zl * X + x_by(-d)]
+        factor = jnp.exp((one[0:TILES, :] - top) * SCALE) * inverse
+        shift = whole_delta * inverse - one[2 * TILES : 3 * TILES, :] / one[TILES : 2 * TILES, :]
+        return as_row(factor), as_row(shift)
+
+    weights = [weigh(d) for d in range(X)]
     top, inverse, row_delta = as_row(top), as_row(inverse), as_row(whole_delta * inverse)
-    weight = jnp.exp((peak - top) * SCALE) * inverse
-
-    class Part:
-        def __init__(self, full, sent, from_x, middle, from_zl, whole):
-            self.full, self.sent, self.from_x = full, sent, from_x
-            self.middle, self.from_zl, self.whole = middle, from_zl, whole
-            self.rows = full.shape[0] // (X * ZL)
-
-        def block(self, to_x, to_zl):
-            return pl.ds(pl.multiple_of((to_x * ZL + to_zl) * self.rows, self.rows), self.rows)
-
-        def put(self, row, part):
-            self.full[row : row + part.shape[0], :] = part
-            self.sent[row : row + part.shape[0], :] = part.astype(BF16)
-
-        def send_x(self):
-            self.at_x = {}
-            for e in (2, 1, 3, 0):
-                to = zl_by(e)
-                self.at_x[e] = [
-                    sems.copy(
-                        self.sent.at[self.block(x_by(d), to), :],
-                        self.from_x.at[d - 1, to],
-                        at(x_=x_by(d)),
-                    )
-                    for d in (2, 1, 3)
-                ]
-
-        def sum_x(self):
-            self.at_zl = []
-            for e in (2, 1, 3, 0):
-                for made in self.at_x[e]:
-                    made.wait_recv()
-                to = zl_by(e)
-                add = self.full[self.block(x, to), :]
-                for i in range(X - 1):
-                    add += self.from_x[i, to].astype(F32)
-                self.middle[to] = add.astype(BF16)
-                if e:
-                    self.at_zl.append(
-                        sems.copy(self.middle.at[to], self.from_zl.at[e - 1], at(zl_=to))
-                    )
-
-        def spread_x(self, e):
-            block = self.whole.at[self.block(x, zl_by(-e)), :]
-            return [sems.copy(block, block, at(x_=x_by(d))) for d in (2, 1, 3)]
-
-        def sum_zl(self):
-            for made in self.at_zl:
+
+    def weighted(own, came):
+        out, grad = None, None
+        for d, (factor, shift) in enumerate(weights):
+            acc, dif = own if d == 0 else came(d - 1)
+            part, part_grad = factor * acc, factor * (dif - shift * acc)
+            out = part if d == 0 else out + part
+            grad = part_grad if d == 0 else grad + part_grad
+        return out, grad * SCALE
+
+    lat_zl = []
+
+    def sum_x(e):
+        for made in lat_x[e]:
+            made.wait_recv()
+        to = zl_by(e)
+        rows = pl.ds(pl.multiple_of((x * ZL + to) * COLS, COLS), COLS)
+
+        def came(i):
+            return lat_r[i, to, 0].astype(F32), lat_r[i, to, 1].astype(F32)
+
+        out, grad = weighted((acc_t[rows, :], dif_t[rows, :]), came)
+        lat_m[to, 0] = out.astype(BF16)
+        lat_m[to, 1] = grad.astype(BF16)
+        if e:
+            lat_zl.append(sems.copy(lat_m.at[to], lat_z.at[e - 1], at(zl_=to)))
+
+    def sum_rope_x():
+        for made in rope_x:
+            made.wait_recv()
+        rows = pl.ds(pl.multiple_of(LATENT + x * RCOLS, RCOLS), RCOLS)
+
+        def came(i):
+            return rope_r[i, 0].astype(F32), rope_r[i, 1].astype(F32)
+
+        _, grad = weighted((acc_t[rows, :], dif_t[rows, :]), came)
+        rope_z[zl] = grad.astype(BF16)
+        block = rope_z.at[zl]
+        return [sems.copy(block, block, at(zl_=zl_by(e))) for e in (2, 1, 3)]
+
+    def block_of(to_x, to_zl):
+        return pl.ds(pl.multiple_of((to_x * ZL + to_zl) * COLS, COLS), COLS)
+
+    def spread_x(e):
+        rows = block_of(x, zl_by(-e))
+        for whole in (abs_a, value_a):
+            block = whole.at[rows, :]
+            for d in (2, 1, 3):
+                at_x[d].append(sems.copy(block, block, at(x_=x_by(d))))
+
+    at_x = {1: [], 2: [], 3: []}
+
+    def sum_zl():
+        for made in lat_zl:
+            made.wait_recv()
+        out = lat_m[zl, 0].astype(F32)
+        grad = lat_m[zl, 1].astype(F32)
+        for i in range(ZL - 1):
+            out += lat_z[i, 0].astype(F32)
+            grad += lat_z[i, 1].astype(F32)
+        rows = block_of(x, zl)
+        abs_a[rows, :] = grad.astype(BF16)
+        value_a[rows, :] = dot(out.astype(BF16), og_exp[...]).astype(BF16)
+        back = {}
+        for e in (2, 1, 3):
+            back[e] = [
+                sems.copy(whole.at[rows, :], whole.at[rows, :], at(zl_=zl_by(e)))
+                for whole in (abs_a, value_a)
+            ]
+        spread_x(0)
+        return back
+
+    def sum_rope_zl(made):
+        for m in made:
+            m.wait_recv()
+        grad = rope_z[0].astype(F32)
+        for i in range(1, ZL):
+            grad += rope_z[i].astype(F32)
+        rope_a[x] = grad.astype(BF16)
+        block = rope_a.at[x]
+        for d in (2, 1, 3):
+            at_x[d].append(sems.copy(block, block, at(x_=x_by(d))))
+
+    def gather_x(back):
+        for e in (1, 3, 2):
+            for made in back[e]:
                 made.wait_recv()
-            add = self.middle[zl].astype(F32)
-            for i in range(ZL - 1):
-                add += self.from_zl[i].astype(F32)
-            own = self.block(x, zl)
-            self.whole[own, :] = add.astype(BF16)
-            block = self.whole.at[own, :]
-            self.back = {e: sems.copy(block, block, at(zl_=zl_by(e))) for e in (2, 1, 3)}
-            self.out = self.spread_x(0)
-
-        def gather_x(self):
-            for e in (1, 3, 2):
-                self.back[e].wait_recv()
-                self.out += self.spread_x(e)
-
-        def done(self, result):
-            for made in self.out:
+            spread_x(e)
+
+    def finish(d):
+        if d:
+            for made in at_x[d]:
                 made.wait_recv()
-            result[...] = self.whole[...]
-
-    value_part = Part(w1f, w1b, w1x, w1m, w1z, w1a)
-    key_part = Part(w2f, w2b, w2x, w2m, w2z, w2a)
-    query_part = Part(w3f, w3b, w3x, w3m, w3z, w3a)
-    scaled = (acc_t[:LATENT, :] * weight).astype(BF16)
-    for h in range(HEADS):
-        cols = slice(h * VHEAD, (h + 1) * VHEAD)
-        value_part.put(h * LATENT, dot(scaled, og_exp[:, cols]))
-    value_part.send_x()
-
-    shift = row_delta - mean
-    factor = weight * SCALE
-    lat = (factor * (dif_t[:LATENT, :] - shift * acc_t[:LATENT, :])).astype(BF16)
-    rope = factor * (dif_t[LATENT:, :] - shift * acc_t[LATENT:, :])
-    for b in range(LATENT // TILE):
-        key_part.put(
-            b * HEADS * NOPE, dot_nt(qn_exp_t[...], lat[b * TILE : (b + 1) * TILE, :])
-        )
-    key_part.send_x()
-    spread = dot(ku_ref[...], lat)
-    head_of = lane & (HEADS - 1)
-    nope = spread[:NOPE, :]
-    for h in range(1, HEADS):
-        nope = jnp.where(head_of == h, spread[h * NOPE : (h + 1) * NOPE, :], nope)
-    for t in range(TILES):
-        cols = slice(t * TILE, (t + 1) * TILE)
-        query_part.put(t * QUERY, jnp.concatenate([nope[:, cols], rope[:, cols]], 0))
-    query_part.put(TILES * QUERY, jnp.zeros((W3 - TILES * QUERY, TILE), F32))
-    query_part.send_x()
+        b = x_by(-d)
+        cols = pl.ds(pl.multiple_of(b * TILE, TILE), TILE)
+        lat = abs_a[cols, :]
+        key_up_out[b] = dot_nt(qn_exp_t[...], lat)
+        return dot(ku_ref[:, cols], lat)
 
     core_sums, y_sums, zh_sums = {}, {}, {}
 
@@ -438,59 +473,61 @@
             sems.copy(c3s.at[1], c3r.at[1], at(zh_=zh_by(-1))),
         ]
 
-    for dz in (2, 1, 3, 0):
-        key_grads(dz)
-    value_part.sum_x()
-    for dz in (2, 1, 3, 0):
-        add_cores(dz)
-    key_part.sum_x()
-    query_part.sum_x()
+    sum_x(2)
+    key_grads(2)
+    sum_x(1)
+    key_grads(1)
+    add_cores(2)
+    key_grads(3)
+    add_cores(1)
+    sum_x(3)
+    key_grads(0)
+    add_cores(3)
+    sum_x(0)
+    rope_zl = sum_rope_x()
+    add_cores(0)
     halves = send_far(add_ys(2))
-    value_part.sum_zl()
+    back = sum_zl()
+    sum_rope_zl(rope_zl)
     up, down, final = add_ys(3), add_ys(1), add_ys(0)
-    key_part.sum_zl()
-    value_part.gather_x()
-    query_part.sum_zl()
+    gather_x(back)
     near = send_near(halves, up, down)
-    key_part.gather_x()
-    query_part.gather_x()
-
+
+    spread = finish(0)
+    for d in (1, 3, 2):
+        spread += finish(d)
+    for b in range(X):
+        query_out[NOPE + b * RCOLS : NOPE + (b + 1) * RCOLS, :] = rope_a[b].astype(F32)
+    head_of = lane & (HEADS - 1)
+    nope = spread[:NOPE, :]
+    for h in range(1, HEADS):
+        nope = jnp.where(head_of == h, spread[h * NOPE : (h + 1) * NOPE, :], nope)
+    query_out[:NOPE, :] = nope
+    value_out[...] = value_a[...]
     for made in near:
         made.wait_recv()
     keys_out[...] = final + c3r[0].astype(F32) + c3r[1].astype(F32)
-    value_part.done(w1_out)
-    key_part.done(w2_out)
-    query_part.done(w3_out)
     for made in sems.started:
         made.wait_send()
 
 
 def unpack(
-    keys_ref, w1_ref, w2_ref, w3_ref,
+    keys_ref, value_ref, key_up_ref, query_ref,
     prompt_out, suffix_out, query_out, key_up_out, value_up_out,
 ):
     prompt_out[0] = keys_ref[:PKEYS, :]
     prompt_out[1] = keys_ref[PKEYS : 2 * PKEYS, :]
     suffix_out[0] = keys_ref[2 * PKEYS :, :]
-    value_up_out[...] = w1_ref[...].astype(F32)
-    for b in range(LATENT // TILE):
-        key_up_out[:, b * TILE : (b + 1) * TILE] = w2_ref[b * 512 : (b + 1) * 512, :].astype(F32)
+    for h in range(HEADS):
+        value_up_out[h * LATENT : (h + 1) * LATENT, :] = value_ref[
+            :, h * VHEAD : (h + 1) * VHEAD
+        ].astype(F32)
+    for b in range(X):
+        key_up_out[:, b * TILE : (b + 1) * TILE] = key_up_ref[b]
     steps = TILE // HEADS
     for t in range(TILES):
-        part = w3_ref[t * QUERY : (t + 1) * QUERY, :].astype(F32).T
+        part = query_ref[:, t * TILE : (t + 1) * TILE].T
         query_out[t * steps : (t + 1) * steps] = part.reshape(steps, HEADS, QUERY)
-
-
-def part_scratch(rows):
-    block = rows // (X * ZL)
-    return (
-        pltpu.VMEM((rows, TILE), F32),
-        pltpu.VMEM((rows, TILE), BF16),
-        pltpu.VMEM((X - 1, ZL, block, TILE), BF16),
-        pltpu.VMEM((ZL, block, TILE), BF16),
-        pltpu.VMEM((ZL - 1, block, TILE), BF16),
-        pltpu.VMEM((rows, TILE), BF16),
-    )
 
 
 def shards(prompt, suffix, queries, key_up, value_up, out_grad, fork_prompt, suffix_length):
@@ -507,9 +544,9 @@
         kernel,
         out_shape=(
             jax.ShapeDtypeStruct((BLOCK, WIDTH), F32),
-            jax.ShapeDtypeStruct((W1, TILE), BF16),
-            jax.ShapeDtypeStruct((W2, TILE), BF16),
-            jax.ShapeDtypeStruct((W3, TILE), BF16),
+            jax.ShapeDtypeStruct((LATENT, HEADS * VHEAD), BF16),
+            jax.ShapeDtypeStruct((X, HEADS * NOPE, TILE), F32),
+            jax.ShapeDtypeStruct((QUERY, ROWS), F32),
         ),
         in_specs=[vmem] * 2 + [hbm] * 4 + [smem] * 2,
         out_specs=(vmem,) * 4,
@@ -537,9 +574,16 @@
             pltpu.VMEM((ZH - 1, BLOCK, WIDTH), BF16),
             pltpu.VMEM((2, BLOCK // 2, WIDTH), BF16),
             pltpu.VMEM((2, BLOCK, WIDTH), BF16),
-            *part_scratch(W1),
-            *part_scratch(W2),
-            *part_scratch(W3),
+            pltpu.VMEM((X, ZL, 2, COLS, ROWS), BF16),
+            pltpu.VMEM((X - 1, ZL, 2, COLS, ROWS), BF16),
+            pltpu.VMEM((ZL, 2, COLS, ROWS), BF16),
+            pltpu.VMEM((ZL - 1, 2, COLS, ROWS), BF16),
+            pltpu.VMEM((X, 2, RCOLS, ROWS), BF16),
+            pltpu.VMEM((X - 1, 2, RCOLS, ROWS), BF16),
+            pltpu.VMEM((ZL, RCOLS, ROWS), BF16),
+            pltpu.VMEM((LATENT, ROWS), BF16),
+            pltpu.VMEM((LATENT, HEADS * VHEAD), BF16),
+            pltpu.VMEM((X, RCOLS, ROWS), BF16),
             pltpu.VMEM((steps, HEADS, QUERY), BF16),
             pltpu.VMEM((HEADS * NOPE, LATENT), BF16),
             pltpu.VMEM((HEADS * LATENT, VHEAD), BF16),

time: 80 us -> 81.3 us (1.016)
  Pallas kernels: 79.2 us -> 80.5 us
    pallas_call x1, Pallas kernels: 77.4 us -> 78.6 us  [shards(): pl.pallas_call(kernel, out_shape=(jax.ShapeDtypeStruct((BLOCK, WIDTH), F3...]
where the time goes in v5:
time: 81.3 us; the launch traced here: 81.1 us
  Pallas kernels  80.5 us (99%)
    pallas_call x1, Pallas kernels, shards(): pl.pallas_call(kernel, out_shape=(jax.ShapeDtypeStruct((BLOCK, WIDTH), F3...  78.6 us
    pallas_call x1, Pallas kernels, shards(): pl.pallas_call(unpack, out_shape=(jax.ShapeDtypeStruct((2, PKEYS, WIDTH),...  1.86 us

profile of v5, /device:TPU:64, one launch (start us, length us, event | category | flops | bytes accessed | tf_op | source)
XLA Modules:
  0.0 81.1 jit_solution(17655084669004094287)
XLA Ops:
  0.6 78.6 %latent_backward.1 = (f32[32,576]{1,0:T(8,128)S(1)}, bf16[512,512]{1,0:T(8,128)(2,1)S(1)}, f32[4,512,128]{2,1,0:T(8,128)S(1)}, f32[192,640]{1,0:T(8,128)S(1)}) custom-call(bf16[2,8,576]{2,1,0:T(8,128)(2,1)} %prompt_ref.1, bf16[1,16,576]{2,1,0:T(8,128)(2,1)} %suffix_ref.1, bf16[160,4,192]{2,1,0:T(4,128)(2,1)} %bitcast.12, bf16[512,512]{1,0:T(8,128)(2,1)} %bitcast.10, ...), custom_call_target="tpu_custom_call" | custom-call | flops 8000000000 | bytes 6000000 | tf_op jit(solution)/shard_map/latent_backward/pallas_call | solution.py:543
  79.3 1.9 %unpack_grads.1 = (f32[2,8,576]{2,1,0:T(8,128)}, f32[1,16,576]{2,1,0:T(8,128)}, f32[160,4,192]{2,1,0:T(4,128)}, f32[512,512]{1,0:T(8,128)}, f32[2048,128]{1,0:T(8,128)}) custom-call(f32[32,576]{1,0:T(8,128)S(1)} %get-tuple-element.14.keys_ref, bf16[512,512]{1,0:T(8,128)(2,1)S(1)} %get-tuple-element.15.value_ref, ...), custom_call_target="tpu_custom_call" | custom-call | tf_op jit(solution)/shard_map/unpack_grads/pallas_call | solution.py:612

commit v6 on v5

--- a/solution.py
+++ b/solution.py
@@ -61,7 +61,7 @@
     keys_out, value_out, key_up_out, query_out,
     keys, qry, qry_t, lgr, lgr_t, og_exp, qn_exp_t, bias, score, pgrad, peaks,
     acc_t, dif_t, kgrad, stat, stat_all, c1s, c1r, c2s, c2r, c3s, c3h, c3r,
-    lat_s, lat_r, lat_m, lat_z, rope_s, rope_r, rope_z, abs_a, value_a, rope_a,
+    far_s, far_r, near_s, near_r, lat_m, lat_z, rope_s, rope_r, rope_z, whole, rope_a,
     q_ref, ku_ref, vu_ref, og_ref, send_sem, recv_sem, load_sem,
 ):
     ctx, sample = lax.axis_index("ctx"), lax.axis_index("sample")
@@ -281,21 +281,23 @@
     stat_all[ctx] = stat[...]
 
     add_sums(state, new, part)
+    half_cols = COLS // 2
+    ORDER = (2, 1, 3, 0)
+    far_x = {}
+    for e in ORDER:
+        to = zl_by(e)
+        for k in range(2):
+            start = (x_by(2) * ZL + to) * COLS + k * half_cols
+            rows = pl.ds(pl.multiple_of(start, half_cols), half_cols)
+            far_s[to, k, 0] = acc_t[rows, :].astype(BF16)
+            far_s[to, k, 1] = dif_t[rows, :].astype(BF16)
+        far_x[e] = [
+            sems.copy(far_s.at[to, k], far_r.at[k, to], at(x_=x_by(1 - 2 * k))) for k in range(2)
+        ]
     for b in range(X):
-        for c in range(ZL):
-            rows = slice((b * ZL + c) * COLS, (b * ZL + c + 1) * COLS)
-            lat_s[b, c, 0] = acc_t[rows, :].astype(BF16)
-            lat_s[b, c, 1] = dif_t[rows, :].astype(BF16)
         rows = slice(LATENT + b * RCOLS, LATENT + (b + 1) * RCOLS)
         rope_s[b, 0] = acc_t[rows, :].astype(BF16)
         rope_s[b, 1] = dif_t[rows, :].astype(BF16)
-    lat_x = {}
-    for e in (2, 1, 3, 0):
-        to = zl_by(e)
-        lat_x[e] = [
-            sems.copy(lat_s.at[x_by(d), to], lat_r.at[d - 1, to], at(x_=x_by(d)))
-            for d in (2, 1, 3)
-        ]
     rope_x = [
         sems.copy(rope_s.at[x_by(d)], rope_r.at[d - 1], at(x_=x_by(d))) for d in (2, 1, 3)
     ]
@@ -324,29 +326,43 @@
     weights = [weigh(d) for d in range(X)]
     top, inverse, row_delta = as_row(top), as_row(inverse), as_row(whole_delta * inverse)
 
-    def weighted(own, came):
-        out, grad = None, None
-        for d, (factor, shift) in enumerate(weights):
-            acc, dif = own if d == 0 else came(d - 1)
-            part, part_grad = factor * acc, factor * (dif - shift * acc)
-            out = part if d == 0 else out + part
-            grad = part_grad if d == 0 else grad + part_grad
-        return out, grad * SCALE
+    def weighted(d, acc, dif):
+        factor, shift = weights[d]
+        return factor * acc, (factor * SCALE) * (dif - shift * acc)
+
+    def block_of(to_x, to_zl):
+        return pl.ds(pl.multiple_of((to_x * ZL + to_zl) * COLS, COLS), COLS)
+
+    near_x = {}
+
+    def send_near_x(e):
+        to = zl_by(e)
+        near_x[e] = []
+        for k in range(2):
+            far_x[e][k].wait_recv()
+            rows = block_of(x_by(1 - 2 * k), to)
+            own = weighted(0, acc_t[rows, :], dif_t[rows, :])
+            came = weighted(1 + 2 * k, far_r[k, to, 0].astype(F32), far_r[k, to, 1].astype(F32))
+            added = slice(k * half_cols, (k + 1) * half_cols)
+            other = slice((1 - k) * half_cols, (2 - k) * half_cols)
+            for i in range(2):
+                near_s[k, to, i, added] = (own[i][added] + came[i]).astype(BF16)
+                near_s[k, to, i, other] = own[i][other].astype(BF16)
+            near_x[e].append(
+                sems.copy(near_s.at[k, to], near_r.at[k, to], at(x_=x_by(1 - 2 * k)))
+            )
 
     lat_zl = []
 
     def sum_x(e):
-        for made in lat_x[e]:
+        for made in near_x[e]:
             made.wait_recv()
         to = zl_by(e)
-        rows = pl.ds(pl.multiple_of((x * ZL + to) * COLS, COLS), COLS)
-
-        def came(i):
-            return lat_r[i, to, 0].astype(F32), lat_r[i, to, 1].astype(F32)
-
-        out, grad = weighted((acc_t[rows, :], dif_t[rows, :]), came)
-        lat_m[to, 0] = out.astype(BF16)
-        lat_m[to, 1] = grad.astype(BF16)
+        rows = block_of(x, to)
+        own = weighted(0, acc_t[rows, :], dif_t[rows, :])
+        for i in range(2):
+            add = own[i] + near_r[0, to, i].astype(F32) + near_r[1, to, i].astype(F32)
+            lat_m[to, i] = add.astype(BF16)
         if e:
             lat_zl.append(sems.copy(lat_m.at[to], lat_z.at[e - 1], at(zl_=to)))
 
@@ -355,25 +371,28 @@
             made.wait_recv()
         rows = pl.ds(pl.multiple_of(LATENT + x * RCOLS, RCOLS), RCOLS)
 
-        def came(i):
-            return rope_r[i, 0].astype(F32), rope_r[i, 1].astype(F32)
-
-        _, grad = weighted((acc_t[rows, :], dif_t[rows, :]), came)
+        grad = weighted(0, acc_t[rows, :], dif_t[rows, :])[1]
+        for d in (1, 2, 3):
+            grad += weighted(d, rope_r[d - 1, 0].astype(F32), rope_r[d - 1, 1].astype(F32))[1]
         rope_z[zl] = grad.astype(BF16)
         block = rope_z.at[zl]
         return [sems.copy(block, block, at(zl_=zl_by(e))) for e in (2, 1, 3)]
 
-    def block_of(to_x, to_zl):
-        return pl.ds(pl.multiple_of((to_x * ZL + to_zl) * COLS, COLS), COLS)
+    to_near = {}
+    to_far = []
 
     def spread_x(e):
-        rows = block_of(x, zl_by(-e))
-        for whole in (abs_a, value_a):
-            block = whole.at[rows, :]
-            for d in (2, 1, 3):
-                at_x[d].append(sems.copy(block, block, at(x_=x_by(d))))
-
-    at_x = {1: [], 2: [], 3: []}
+        block = whole.at[block_of(x, zl_by(-e)), :]
+        to_near[e] = [sems.copy(block, block, at(x_=x_by(1 - 2 * k))) for k in range(2)]
+
+    def forward_x(e):
+        for k in range(2):
+            to_near[e][k].wait_recv()
+            start = (x_by(2 * k - 1) * ZL + zl_by(-e)) * COLS + k * half_cols
+            block = whole.at[pl.ds(pl.multiple_of(start, half_cols), half_cols), :]
+            to_far.append(sems.copy(block, block, at(x_=x_by(1 - 2 * k))))
+
+    rope_far = []
 
     def sum_zl():
         for made in lat_zl:
@@ -384,14 +403,10 @@
             out += lat_z[i, 0].astype(F32)
             grad += lat_z[i, 1].astype(F32)
         rows = block_of(x, zl)
-        abs_a[rows, :] = grad.astype(BF16)
-        value_a[rows, :] = dot(out.astype(BF16), og_exp[...]).astype(BF16)
-        back = {}
-        for e in (2, 1, 3):
-            back[e] = [
-                sems.copy(whole.at[rows, :], whole.at[rows, :], at(zl_=zl_by(e)))
-                for whole in (abs_a, value_a)
-            ]
+        whole[rows, :ROWS] = grad.astype(BF16)
+        whole[rows, ROWS:] = dot(out.astype(BF16), og_exp[...]).astype(BF16)
+        block = whole.at[rows, :]
+        back = {e: sems.copy(block, block, at(zl_=zl_by(e))) for e in (2, 1, 3)}
         spread_x(0)
         return back
 
@@ -404,21 +419,21 @@
         rope_a[x] = grad.astype(BF16)
         block = rope_a.at[x]
         for d in (2, 1, 3):
-            at_x[d].append(sems.copy(block, block, at(x_=x_by(d))))
+            rope_far.append(sems.copy(block, block, at(x_=x_by(d))))
 
     def gather_x(back):
+        done = 0
         for e in (1, 3, 2):
-            for made in back[e]:
-                made.wait_recv()
+            back[e].wait_recv()
             spread_x(e)
+            forward_x(done)
+            done = e
+        forward_x(done)
 
     def finish(d):
-        if d:
-            for made in at_x[d]:
-                made.wait_recv()
         b = x_by(-d)
         cols = pl.ds(pl.multiple_of(b * TILE, TILE), TILE)
-        lat = abs_a[cols, :]
+        lat = whole[cols, :ROWS]
         key_up_out[b] = dot_nt(qn_exp_t[...], lat)
         return dot(ku_ref[:, cols], lat)
 
@@ -473,18 +488,20 @@
             sems.copy(c3s.at[1], c3r.at[1], at(zh_=zh_by(-1))),
         ]
 
-    sum_x(2)
+    for e in ORDER:
+        send_near_x(e)
     key_grads(2)
-    sum_x(1)
     key_grads(1)
     add_cores(2)
+    sum_x(2)
     key_grads(3)
     add_cores(1)
-    sum_x(3)
+    sum_x(1)
     key_grads(0)
     add_cores(3)
+    sum_x(3)
+    rope_zl = sum_rope_x()
     sum_x(0)
-    rope_zl = sum_rope_x()
     add_cores(0)
     halves = send_far(add_ys(2))
     back = sum_zl()
@@ -493,9 +510,12 @@
     gather_x(back)
     near = send_near(halves, up, down)
 
-    spread = finish(0)
-    for d in (1, 3, 2):
-        spread += finish(d)
+    spread = finish(0) + finish(1) + finish(3)
+    for made in to_far:
+        made.wait_recv()
+    spread += finish(2)
+    for made in rope_far:
+        made.wait_recv()
     for b in range(X):
         query_out[NOPE + b * RCOLS : NOPE + (b + 1) * RCOLS, :] = rope_a[b].astype(F32)
     head_of = lane & (HEADS - 1)
@@ -503,7 +523,7 @@
     for h in range(1, HEADS):
         nope = jnp.where(head_of == h, spread[h * NOPE : (h + 1) * NOPE, :], nope)
     query_out[:NOPE, :] = nope
-    value_out[...] = value_a[...]
+    value_out[...] = whole[:, ROWS:]
     for made in near:
         made.wait_recv()
     keys_out[...] = final + c3r[0].astype(F32) + c3r[1].astype(F32)
@@ -574,15 +594,16 @@
             pltpu.VMEM((ZH - 1, BLOCK, WIDTH), BF16),
             pltpu.VMEM((2, BLOCK // 2, WIDTH), BF16),
             pltpu.VMEM((2, BLOCK, WIDTH), BF16),
-            pltpu.VMEM((X, ZL, 2, COLS, ROWS), BF16),
-            pltpu.VMEM((X - 1, ZL, 2, COLS, ROWS), BF16),
+            pltpu.VMEM((ZL, 2, 2, COLS // 2, ROWS), BF16),
+            pltpu.VMEM((2, ZL, 2, COLS // 2, ROWS), BF16),
+            pltpu.VMEM((2, ZL, 2, COLS, ROWS), BF16),
+            pltpu.VMEM((2, ZL, 2, COLS, ROWS), BF16),
             pltpu.VMEM((ZL, 2, COLS, ROWS), BF16),
             pltpu.VMEM((ZL - 1, 2, COLS, ROWS), BF16),
             pltpu.VMEM((X, 2, RCOLS, ROWS), BF16),
             pltpu.VMEM((X - 1, 2, RCOLS, ROWS), BF16),
             pltpu.VMEM((ZL, RCOLS, ROWS), BF16),
-            pltpu.VMEM((LATENT, ROWS), BF16),
-            pltpu.VMEM((LATENT, HEADS * VHEAD), BF16),
+            pltpu.VMEM((LATENT, ROWS + HEADS * VHEAD), BF16),
             pltpu.VMEM((X, RCOLS, ROWS), BF16),
             pltpu.VMEM((steps, HEADS, QUERY), BF16),
             pltpu.VMEM((HEADS * NOPE, LATENT), BF16),

time: 81.3 us -> 80.5 us (level)
    pallas_call x1, Pallas kernels: 78.6 us -> 77.8 us  [shards(): pl.pallas_call(kernel, out_shape=(jax.ShapeDtypeStruct((BLOCK, WIDTH), F3...]
where the time goes in v6:
time: 80.5 us; the launch traced here: 80.3 us
  Pallas kernels  79.7 us (99%)
    pallas_call x1, Pallas kernels, shards(): pl.pallas_call(kernel, out_shape=(jax.ShapeDtypeStruct((BLOCK, WIDTH), F3...  77.8 us
    pallas_call x1, Pallas kernels, shards(): pl.pallas_call(unpack, out_shape=(jax.ShapeDtypeStruct((2, PKEYS, WIDTH),...  1.86 us

profile of v6, /device:TPU:64, one launch (start us, length us, event | category | flops | bytes accessed | tf_op | source)
XLA Modules:
  0.0 80.3 jit_solution(5607976540867399327)
XLA Ops:
  0.6 77.8 %latent_backward.1 = (f32[32,576]{1,0:T(8,128)S(1)}, bf16[512,512]{1,0:T(8,128)(2,1)S(1)}, f32[4,512,128]{2,1,0:T(8,128)S(1)}, f32[192,640]{1,0:T(8,128)S(1)}) custom-call(bf16[2,8,576]{2,1,0:T(8,128)(2,1)} %prompt_ref.1, bf16[1,16,576]{2,1,0:T(8,128)(2,1)} %suffix_ref.1, bf16[160,4,192]{2,1,0:T(4,128)(2,1)} %bitcast.12, bf16[512,512]{1,0:T(8,128)(2,1)} %bitcast.10, ...), custom_call_target="tpu_custom_call" | custom-call | flops 8000000000 | bytes 6000000 | tf_op jit(solution)/shard_map/latent_backward/pallas_call | solution.py:563
  78.4 1.9 %unpack_grads.1 = (f32[2,8,576]{2,1,0:T(8,128)}, f32[1,16,576]{2,1,0:T(8,128)}, f32[160,4,192]{2,1,0:T(4,128)}, f32[512,512]{1,0:T(8,128)}, f32[2048,128]{1,0:T(8,128)}) custom-call(f32[32,576]{1,0:T(8,128)S(1)} %get-tuple-element.14.keys_ref, bf16[512,512]{1,0:T(8,128)(2,1)S(1)} %get-tuple-element.15.value_ref, ...), custom_call_target="tpu_custom_call" | custom-call | tf_op jit(solution)/shard_map/unpack_grads/pallas_call | solution.py:633

commit v7 on v6

--- a/solution.py
+++ b/solution.py
@@ -25,6 +25,7 @@
 KEYS = CORE * Y * BLOCK
 SCALE = QUERY**-0.5
 COLS = LATENT // (X * ZL)
+GROUP = COLS // 2
 RCOLS = ROPE // X
 
 
@@ -281,19 +282,28 @@
     stat_all[ctx] = stat[...]
 
     add_sums(state, new, part)
-    half_cols = COLS // 2
     ORDER = (2, 1, 3, 0)
+    FAR_LANES = (slice(0, 3 * TILE), slice(3 * TILE, ROWS))
+    OUT_LANES = (slice(0, ROWS), slice(ROWS, ROWS + HEADS * VHEAD))
+
+    def block_of(to_x, to_zl, g):
+        return pl.ds(pl.multiple_of((to_x * ZL + to_zl) * COLS + g * GROUP, GROUP), GROUP)
+
     far_x = {}
-    for e in ORDER:
-        to = zl_by(e)
-        for k in range(2):
-            start = (x_by(2) * ZL + to) * COLS + k * half_cols
-            rows = pl.ds(pl.multiple_of(start, half_cols), half_cols)
-            far_s[to, k, 0] = acc_t[rows, :].astype(BF16)
-            far_s[to, k, 1] = dif_t[rows, :].astype(BF16)
-        far_x[e] = [
-            sems.copy(far_s.at[to, k], far_r.at[k, to], at(x_=x_by(1 - 2 * k))) for k in range(2)
-        ]
+    for g in range(2):
+        for e in ORDER:
+            to = zl_by(e)
+            rows = block_of(x_by(2), to, g)
+            far_s[to, g, 0] = acc_t[rows, :].astype(BF16)
+            far_s[to, g, 1] = dif_t[rows, :].astype(BF16)
+            far_x[e, g] = [
+                sems.copy(
+                    far_s.at[to, g, :, :, FAR_LANES[k]],
+                    far_r.at[to, g, :, :, FAR_LANES[k]],
+                    at(x_=x_by(1 - 2 * k)),
+                )
+                for k in range(2)
+            ]
     for b in range(X):
         rows = slice(LATENT + b * RCOLS, LATENT + (b + 1) * RCOLS)
         rope_s[b, 0] = acc_t[rows, :].astype(BF16)
@@ -326,45 +336,46 @@
     weights = [weigh(d) for d in range(X)]
     top, inverse, row_delta = as_row(top), as_row(inverse), as_row(whole_delta * inverse)
 
-    def weighted(d, acc, dif):
-        factor, shift = weights[d]
+    def weighted(d, acc, dif, lanes=slice(0, ROWS)):
+        factor, shift = weights[d][0][:, lanes], weights[d][1][:, lanes]
         return factor * acc, (factor * SCALE) * (dif - shift * acc)
 
-    def block_of(to_x, to_zl):
-        return pl.ds(pl.multiple_of((to_x * ZL + to_zl) * COLS, COLS), COLS)
-
     near_x = {}
 
-    def send_near_x(e):
+    def send_near_x(e, g):
         to = zl_by(e)
-        near_x[e] = []
+        near_x[e, g] = []
         for k in range(2):
-            far_x[e][k].wait_recv()
-            rows = block_of(x_by(1 - 2 * k), to)
+            far_x[e, g][k].wait_recv()
+            rows = block_of(x_by(1 - 2 * k), to, g)
             own = weighted(0, acc_t[rows, :], dif_t[rows, :])
-            came = weighted(1 + 2 * k, far_r[k, to, 0].astype(F32), far_r[k, to, 1].astype(F32))
-            added = slice(k * half_cols, (k + 1) * half_cols)
-            other = slice((1 - k) * half_cols, (2 - k) * half_cols)
+            added, other = FAR_LANES[k], FAR_LANES[1 - k]
+            came = weighted(
+                1 + 2 * k,
+                far_r[to, g, 0, :, added].astype(F32),
+                far_r[to, g, 1, :, added].astype(F32),
+                added,
+            )
             for i in range(2):
-                near_s[k, to, i, added] = (own[i][added] + came[i]).astype(BF16)
-                near_s[k, to, i, other] = own[i][other].astype(BF16)
-            near_x[e].append(
-                sems.copy(near_s.at[k, to], near_r.at[k, to], at(x_=x_by(1 - 2 * k)))
+                near_s[k, to, g, i, :, added] = (own[i][:, added] + came[i]).astype(BF16)
+                near_s[k, to, g, i, :, other] = own[i][:, other].astype(BF16)
+            near_x[e, g].append(
+                sems.copy(near_s.at[k, to, g], near_r.at[k, to, g], at(x_=x_by(1 - 2 * k)))
             )
 
-    lat_zl = []
-
-    def sum_x(e):
-        for made in near_x[e]:
+    lat_zl = [[], []]
+
+    def sum_x(e, g):
+        for made in near_x[e, g]:
             made.wait_recv()
         to = zl_by(e)
-        rows = block_of(x, to)
+        rows = block_of(x, to, g)
         own = weighted(0, acc_t[rows, :], dif_t[rows, :])
         for i in range(2):
-            add = own[i] + near_r[0, to, i].astype(F32) + near_r[1, to, i].astype(F32)
-            lat_m[to, i] = add.astype(BF16)
+            add = own[i] + near_r[0, to, g, i].astype(F32) + near_r[1, to, g, i].astype(F32)
+            lat_m[to, g, i] = add.astype(BF16)
         if e:
-            lat_zl.append(sems.copy(lat_m.at[to], lat_z.at[e - 1], at(zl_=to)))
+            lat_zl[g].append(sems.copy(lat_m.at[to, g], lat_z.at[e - 1, g], at(zl_=to)))
 
     def sum_rope_x():
         for made in rope_x:
@@ -381,33 +392,32 @@
     to_near = {}
     to_far = []
 
-    def spread_x(e):
-        block = whole.at[block_of(x, zl_by(-e)), :]
-        to_near[e] = [sems.copy(block, block, at(x_=x_by(1 - 2 * k))) for k in range(2)]
-
-    def forward_x(e):
+    def spread_x(e, g):
+        block = whole.at[block_of(x, zl_by(-e), g), :]
+        to_near[e, g] = [sems.copy(block, block, at(x_=x_by(1 - 2 * k))) for k in range(2)]
+
+    def forward_x(e, g):
         for k in range(2):
-            to_near[e][k].wait_recv()
-            start = (x_by(2 * k - 1) * ZL + zl_by(-e)) * COLS + k * half_cols
-            block = whole.at[pl.ds(pl.multiple_of(start, half_cols), half_cols), :]
+            to_near[e, g][k].wait_recv()
+            block = whole.at[block_of(x_by(2 * k - 1), zl_by(-e), g), OUT_LANES[k]]
             to_far.append(sems.copy(block, block, at(x_=x_by(1 - 2 * k))))
 
     rope_far = []
 
-    def sum_zl():
-        for made in lat_zl:
+    def sum_zl(g):
+        for made in lat_zl[g]:
             made.wait_recv()
-        out = lat_m[zl, 0].astype(F32)
-        grad = lat_m[zl, 1].astype(F32)
+        out = lat_m[zl, g, 0].astype(F32)
+        grad = lat_m[zl, g, 1].astype(F32)
         for i in range(ZL - 1):
-            out += lat_z[i, 0].astype(F32)
-            grad += lat_z[i, 1].astype(F32)
-        rows = block_of(x, zl)
+            out += lat_z[i, g, 0].astype(F32)
+            grad += lat_z[i, g, 1].astype(F32)
+        rows = block_of(x, zl, g)
         whole[rows, :ROWS] = grad.astype(BF16)
         whole[rows, ROWS:] = dot(out.astype(BF16), og_exp[...]).astype(BF16)
         block = whole.at[rows, :]
         back = {e: sems.copy(block, block, at(zl_=zl_by(e))) for e in (2, 1, 3)}
-        spread_x(0)
+        spread_x(0, g)
         return back
 
     def sum_rope_zl(made):
@@ -421,14 +431,13 @@
         for d in (2, 1, 3):
             rope_far.append(sems.copy(block, block, at(x_=x_by(d))))
 
-    def gather_x(back):
+    def gather_x(back, g):
         done = 0
         for e in (1, 3, 2):
             back[e].wait_recv()
-            spread_x(e)
-            forward_x(done)
+            spread_x(e, g)
+            forward_x(done, g)
             done = e
-        forward_x(done)
 
     def finish(d):
         b = x_by(-d)
@@ -488,27 +497,32 @@
             sems.copy(c3s.at[1], c3r.at[1], at(zh_=zh_by(-1))),
         ]
 
+    for g in range(2):
+        for e in ORDER:
+            send_near_x(e, g)
+    key_grads(2)
     for e in ORDER:
-        send_near_x(e)
-    key_grads(2)
+        sum_x(e, 0)
     key_grads(1)
     add_cores(2)
-    sum_x(2)
+    for e in ORDER:
+        sum_x(e, 1)
+    rope_zl = sum_rope_x()
     key_grads(3)
     add_cores(1)
-    sum_x(1)
     key_grads(0)
     add_cores(3)
-    sum_x(3)
-    rope_zl = sum_rope_x()
-    sum_x(0)
+    back_0 = sum_zl(0)
     add_cores(0)
     halves = send_far(add_ys(2))
-    back = sum_zl()
+    back_1 = sum_zl(1)
     sum_rope_zl(rope_zl)
+    gather_x(back_0, 0)
     up, down, final = add_ys(3), add_ys(1), add_ys(0)
-    gather_x(back)
     near = send_near(halves, up, down)
+    gather_x(back_1, 1)
+    forward_x(2, 0)
+    forward_x(2, 1)
 
     spread = finish(0) + finish(1) + finish(3)
     for made in to_far:
@@ -553,7 +567,7 @@
 def shards(prompt, suffix, queries, key_up, value_up, out_grad, fork_prompt, suffix_length):
     vmem = pl.BlockSpec(memory_space=pltpu.VMEM)
     smem = pl.BlockSpec(memory_space=pltpu.SMEM)
-    copies = 152
+    copies = 184
     hbm = pl.BlockSpec(memory_space=pltpu.HBM)
 
     def in_hbm(v):
@@ -594,12 +608,12 @@
             pltpu.VMEM((ZH - 1, BLOCK, WIDTH), BF16),
             pltpu.VMEM((2, BLOCK // 2, WIDTH), BF16),
             pltpu.VMEM((2, BLOCK, WIDTH), BF16),
-            pltpu.VMEM((ZL, 2, 2, COLS // 2, ROWS), BF16),
-            pltpu.VMEM((2, ZL, 2, COLS // 2, ROWS), BF16),
-            pltpu.VMEM((2, ZL, 2, COLS, ROWS), BF16),
-            pltpu.VMEM((2, ZL, 2, COLS, ROWS), BF16),
-            pltpu.VMEM((ZL, 2, COLS, ROWS), BF16),
-            pltpu.VMEM((ZL - 1, 2, COLS, ROWS), BF16),
+            pltpu.VMEM((ZL, 2, 2, GROUP, ROWS), BF16),
+            pltpu.VMEM((ZL, 2, 2, GROUP, ROWS), BF16),
+            pltpu.VMEM((2, ZL, 2, 2, GROUP, ROWS), BF16),
+            pltpu.VMEM((2, ZL, 2, 2, GROUP, ROWS), BF16),
+            pltpu.VMEM((ZL, 2, 2, GROUP, ROWS), BF16),
+            pltpu.VMEM((ZL - 1, 2, 2, GROUP, ROWS), BF16),
             pltpu.VMEM((X, 2, RCOLS, ROWS), BF16),
             pltpu.VMEM((X - 1, 2, RCOLS, ROWS), BF16),
             pltpu.VMEM((ZL, RCOLS, ROWS), BF16),

time: 80.5 us -> 80.2 us (level)
  the two profiles are of different devices: /device:TPU:64 before, /device:TPU:32 now
where the time goes in v7:
time: 80.2 us; the launch traced here: 80 us
  Pallas kernels  79.3 us (99%)
    pallas_call x1, Pallas kernels, shards(): pl.pallas_call(kernel, out_shape=(jax.ShapeDtypeStruct((BLOCK, WIDTH), F3...  77.5 us
    pallas_call x1, Pallas kernels, shards(): pl.pallas_call(unpack, out_shape=(jax.ShapeDtypeStruct((2, PKEYS, WIDTH),...  1.86 us

profile of v7, /device:TPU:32, one launch (start us, length us, event | category | flops | bytes accessed | tf_op | source)
XLA Modules:
  0.0 80.0 jit_solution(5086483345358226862)
XLA Ops:
  0.6 77.5 %latent_backward.1 = (f32[32,576]{1,0:T(8,128)S(1)}, bf16[512,512]{1,0:T(8,128)(2,1)S(1)}, f32[4,512,128]{2,1,0:T(8,128)S(1)}, f32[192,640]{1,0:T(8,128)S(1)}) custom-call(bf16[2,8,576]{2,1,0:T(8,128)(2,1)} %prompt_ref.1, bf16[1,16,576]{2,1,0:T(8,128)(2,1)} %suffix_ref.1, bf16[160,4,192]{2,1,0:T(4,128)(2,1)} %bitcast.12, bf16[512,512]{1,0:T(8,128)(2,1)} %bitcast.10, ...), custom_call_target="tpu_custom_call" | custom-call | flops 8000000000 | bytes 6000000 | tf_op jit(solution)/shard_map/latent_backward/pallas_call | solution.py:577
  78.1 1.9 %unpack_grads.1 = (f32[2,8,576]{2,1,0:T(8,128)}, f32[1,16,576]{2,1,0:T(8,128)}, f32[160,4,192]{2,1,0:T(4,128)}, f32[512,512]{1,0:T(8,128)}, f32[2048,128]{1,0:T(8,128)}) custom-call(f32[32,576]{1,0:T(8,128)S(1)} %get-tuple-element.14.keys_ref, bf16[512,512]{1,0:T(8,128)(2,1)S(1)} %get-tuple-element.15.value_ref, ...), custom_call_target="tpu_custom_call" | custom-call | tf_op jit(solution)/shard_map/unpack_grads/pallas_call | solution.py:647

commit v8 on v7

--- a/solution.py
+++ b/solution.py
@@ -58,12 +58,13 @@
 
 
 def kernel(
-    prompt_ref, suffix_ref, q_any, ku_any, vu_any, og_any, fork_ref, length_ref,
+    prompt_any, suffix_any, q_any, ku_any, vu_any, og_any, fork_any, length_any,
     keys_out, value_out, key_up_out, query_out,
     keys, qry, qry_t, lgr, lgr_t, og_exp, qn_exp_t, bias, score, pgrad, peaks,
     acc_t, dif_t, kgrad, stat, stat_all, c1s, c1r, c2s, c2r, c3s, c3h, c3r,
     far_s, far_r, near_s, near_r, lat_m, lat_z, rope_s, rope_r, rope_z, whole, rope_a,
-    q_ref, ku_ref, vu_ref, og_ref, send_sem, recv_sem, load_sem,
+    prompt_ref, suffix_ref, q_ref, ku_ref, vu_ref, og_ref, fork_ref, length_ref,
+    send_sem, recv_sem, load_sem,
 ):
     ctx, sample = lax.axis_index("ctx"), lax.axis_index("sample")
     zl, x = ctx // X, ctx % X
@@ -87,23 +88,26 @@
         return (zl + d + ZL) % ZL
 
     sems = Sems(send_sem, recv_sem)
-    loads = [
-        pltpu.make_async_copy(src, dst, load_sem.at[k])
-        for k, (src, dst) in enumerate(
-            ((q_any, q_ref), (ku_any, ku_ref), (vu_any, vu_ref), (og_any, og_ref))
-        )
-    ]
-    for made in loads:
+    pairs = (
+        (prompt_any, prompt_ref), (suffix_any, suffix_ref), (q_any, q_ref), (ku_any, ku_ref),
+        (og_any, og_ref), (vu_any, vu_ref), (fork_any, fork_ref), (length_any, length_ref),
+    )
+    loads = [pltpu.make_async_copy(*pair, load_sem.at[k]) for k, pair in enumerate(pairs)]
+    for made in loads[:2]:
         made.start()
 
-    partners = [sibling]
-    partners += [at(zh_=zh_by(d)) for d in (1, -1)]
-    partners += [at(y_=y_by(d)) for d in range(1, Y)]
-    partners += [at(y_=y_by(d), core_=1 - core) for d in range(1, Y)]
-    partners += [at(zl_=zl_by(a), x_=x_by(b)) for a in range(ZL) for b in range(X) if a + b]
+    partners = [at(zh_=zh_by(d)) for d in (1, -1)]
+    partners += [at(zl_=zl_by(a), x_=x_by(b)) for a in (2, 1, 3, 0) for b in (2, 1, 3, 0) if a + b]
+    partners += [at(y_=y_by(d)) for d in (2, 1, 3)]
+    partners += [at(y_=y_by(d), core_=1 - core) for d in (2, 1, 3)]
+    partners += [sibling]
     barrier = pltpu.get_barrier_semaphore()
     for device in partners:
         pl.semaphore_signal(barrier, inc=1, device_id=device, device_id_type=MESH)
+    for made in loads[2:]:
+        made.start()
+    for made in loads[:2]:
+        made.wait()
     own = jnp.concatenate(
         [prompt_ref[0].astype(F32), prompt_ref[1].astype(F32), suffix_ref[0].astype(F32)], 0
     ).astype(BF16)
@@ -175,7 +179,7 @@
         lgr_t[:, rows] = grad.T
         return carry
 
-    for made in loads:
+    for made in loads[2:]:
         made.wait()
     lax.fori_loop(0, 2, project, 0)
     relay(1, pl.ds(0, half))
@@ -566,7 +570,6 @@
 
 def shards(prompt, suffix, queries, key_up, value_up, out_grad, fork_prompt, suffix_length):
     vmem = pl.BlockSpec(memory_space=pltpu.VMEM)
-    smem = pl.BlockSpec(memory_space=pltpu.SMEM)
     copies = 184
     hbm = pl.BlockSpec(memory_space=pltpu.HBM)
 
@@ -582,7 +585,7 @@
             jax.ShapeDtypeStruct((X, HEADS * NOPE, TILE), F32),
             jax.ShapeDtypeStruct((QUERY, ROWS), F32),
         ),
-        in_specs=[vmem] * 2 + [hbm] * 4 + [smem] * 2,
+        in_specs=[hbm] * 8,
         out_specs=(vmem,) * 4,
         scratch_shapes=[
             pltpu.VMEM((ZH, CORE, Y, BLOCK, WIDTH), BF16),
@@ -619,13 +622,17 @@
             pltpu.VMEM((ZL, RCOLS, ROWS), BF16),
             pltpu.VMEM((LATENT, ROWS + HEADS * VHEAD), BF16),
             pltpu.VMEM((X, RCOLS, ROWS), BF16),
+            pltpu.VMEM((2, PKEYS, WIDTH), BF16),
+            pltpu.VMEM((1, SKEYS, WIDTH), BF16),
             pltpu.VMEM((steps, HEADS, QUERY), BF16),
             pltpu.VMEM((HEADS * NOPE, LATENT), BF16),
             pltpu.VMEM((HEADS * LATENT, VHEAD), BF16),
             pltpu.VMEM((steps, HEADS, VHEAD), BF16),
+            pltpu.SMEM((FORKS,), jnp.int32),
+            pltpu.SMEM((FORKS,), jnp.int32),
             pltpu.SemaphoreType.DMA((copies,)),
             pltpu.SemaphoreType.DMA((copies,)),
-            pltpu.SemaphoreType.DMA((4,)),
+            pltpu.SemaphoreType.DMA((8,)),
         ],
         compiler_params=pltpu.CompilerParams(
             collective_id=0, has_side_effects=True, vmem_limit_bytes=42 << 20

time: 80.2 us -> 79.3 us (0.989)
    pallas_call x1, Pallas kernels: 77.5 us -> 76.6 us  [shards(): pl.pallas_call(kernel, out_shape=(jax.ShapeDtypeStruct((BLOCK, WIDTH), F3...]
where the time goes in v8:
time: 79.3 us; the launch traced here: 79.1 us
  Pallas kernels  78.5 us (99%)
    pallas_call x1, Pallas kernels, shards(): pl.pallas_call(kernel, out_shape=(jax.ShapeDtypeStruct((BLOCK, WIDTH), F3...  76.6 us
    pallas_call x1, Pallas kernels, shards(): pl.pallas_call(unpack, out_shape=(jax.ShapeDtypeStruct((2, PKEYS, WIDTH),...  1.86 us

profile of v8, /device:TPU:32, one launch (start us, length us, event | category | flops | bytes accessed | tf_op | source)
XLA Modules:
  0.0 79.1 jit_solution(6896603516588622509)
XLA Ops:
  0.6 76.6 %latent_backward.1 = (f32[32,576]{1,0:T(8,128)S(1)}, bf16[512,512]{1,0:T(8,128)(2,1)S(1)}, f32[4,512,128]{2,1,0:T(8,128)S(1)}, f32[192,640]{1,0:T(8,128)S(1)}) custom-call(bf16[2,8,576]{2,1,0:T(8,128)(2,1)} %prompt_any.1, bf16[1,16,576]{2,1,0:T(8,128)(2,1)} %suffix_any.1, bf16[160,4,192]{2,1,0:T(4,128)(2,1)} %bitcast.12, bf16[512,512]{1,0:T(8,128)(2,1)} %bitcast.10, ...), custom_call_target="tpu_custom_call" | custom-call | flops 8000000000 | bytes 6000000 | tf_op jit(solution)/shard_map/latent_backward/pallas_call | solution.py:580
  77.3 1.9 %unpack_grads.1 = (f32[2,8,576]{2,1,0:T(8,128)}, f32[1,16,576]{2,1,0:T(8,128)}, f32[160,4,192]{2,1,0:T(4,128)}, f32[512,512]{1,0:T(8,128)}, f32[2048,128]{1,0:T(8,128)}) custom-call(f32[32,576]{1,0:T(8,128)S(1)} %get-tuple-element.14.keys_ref, bf16[512,512]{1,0:T(8,128)(2,1)S(1)} %get-tuple-element.15.value_ref, ...), custom_call_target="tpu_custom_call" | custom-call | tf_op jit(solution)/shard_map/unpack_grads/pallas_call | solution.py:654

commit v9 on v8

--- a/solution.py
+++ b/solution.py
@@ -40,6 +40,10 @@
 class Sems:
     def __init__(self, send, recv):
         self.send, self.recv, self.used, self.started = send, recv, 0, []
+
+    def drain(self, kept):
+        while len(self.started) > kept:
+            self.started.pop(0).wait_send()
 
     def copy(self, src, dst, device):
         k = self.used
@@ -443,12 +447,19 @@
             forward_x(done, g)
             done = e
 
+    head_of = lane & (HEADS - 1)
+
     def finish(d):
         b = x_by(-d)
         cols = pl.ds(pl.multiple_of(b * TILE, TILE), TILE)
         lat = whole[cols, :ROWS]
         key_up_out[b] = dot_nt(qn_exp_t[...], lat)
-        return dot(ku_ref[:, cols], lat)
+        value_out[cols, :] = whole[cols, ROWS:]
+        spread = dot(ku_ref[:, cols], lat)
+        nope = spread[:NOPE, :]
+        for h in range(1, HEADS):
+            nope = jnp.where(head_of == h, spread[h * NOPE : (h + 1) * NOPE, :], nope)
+        return nope
 
     core_sums, y_sums, zh_sums = {}, {}, {}
 
@@ -501,6 +512,7 @@
             sems.copy(c3s.at[1], c3r.at[1], at(zh_=zh_by(-1))),
         ]
 
+    early = sems.used
     for g in range(2):
         for e in ORDER:
             send_near_x(e, g)
@@ -519,7 +531,9 @@
     back_0 = sum_zl(0)
     add_cores(0)
     halves = send_far(add_ys(2))
+    sems.drain(sems.used - early)
     back_1 = sum_zl(1)
+    middle = sems.used
     sum_rope_zl(rope_zl)
     gather_x(back_0, 0)
     up, down, final = add_ys(3), add_ys(1), add_ys(0)
@@ -527,45 +541,49 @@
     gather_x(back_1, 1)
     forward_x(2, 0)
     forward_x(2, 1)
-
-    spread = finish(0) + finish(1) + finish(3)
-    for made in to_far:
-        made.wait_recv()
-    spread += finish(2)
+    sems.drain(sems.used - middle)
+
+    nope = finish(0) + finish(1) + finish(3)
     for made in rope_far:
         made.wait_recv()
     for b in range(X):
         query_out[NOPE + b * RCOLS : NOPE + (b + 1) * RCOLS, :] = rope_a[b].astype(F32)
-    head_of = lane & (HEADS - 1)
-    nope = spread[:NOPE, :]
-    for h in range(1, HEADS):
-        nope = jnp.where(head_of == h, spread[h * NOPE : (h + 1) * NOPE, :], nope)
-    query_out[:NOPE, :] = nope
-    value_out[...] = whole[:, ROWS:]
+    for made in to_far:
+        made.wait_recv()
+    query_out[:NOPE, :] = nope + finish(2)
     for made in near:
         made.wait_recv()
     keys_out[...] = final + c3r[0].astype(F32) + c3r[1].astype(F32)
-    for made in sems.started:
-        made.wait_send()
+    sems.drain(0)
 
 
 def unpack(
     keys_ref, value_ref, key_up_ref, query_ref,
     prompt_out, suffix_out, query_out, key_up_out, value_up_out,
+    value_f, query_f, sem,
 ):
+    copies = []
+
+    def put(src, dst):
+        made = pltpu.make_async_copy(src, dst, sem.at[len(copies)])
+        made.start()
+        copies.append(made)
+
+    for b in range(X):
+        put(key_up_ref.at[b], key_up_out.at[:, pl.ds(b * TILE, TILE)])
+    for h in range(HEADS):
+        value_f[h] = value_ref[:, h * VHEAD : (h + 1) * VHEAD].astype(F32)
+        put(value_f.at[h], value_up_out.at[pl.ds(h * LATENT, LATENT), :])
     prompt_out[0] = keys_ref[:PKEYS, :]
     prompt_out[1] = keys_ref[PKEYS : 2 * PKEYS, :]
     suffix_out[0] = keys_ref[2 * PKEYS :, :]
-    for h in range(HEADS):
-        value_up_out[h * LATENT : (h + 1) * LATENT, :] = value_ref[
-            :, h * VHEAD : (h + 1) * VHEAD
-        ].astype(F32)
-    for b in range(X):
-        key_up_out[:, b * TILE : (b + 1) * TILE] = key_up_ref[b]
     steps = TILE // HEADS
     for t in range(TILES):
         part = query_ref[:, t * TILE : (t + 1) * TILE].T
-        query_out[t * steps : (t + 1) * steps] = part.reshape(steps, HEADS, QUERY)
+        query_f[t] = part.reshape(steps, HEADS, QUERY)
+        put(query_f.at[t], query_out.at[pl.ds(t * steps, steps)])
+    for made in copies:
+        made.wait()
 
 
 def shards(prompt, suffix, queries, key_up, value_up, out_grad, fork_prompt, suffix_length):
@@ -661,7 +679,12 @@
             jax.ShapeDtypeStruct((HEADS * LATENT, VHEAD), F32),
         ),
         in_specs=[vmem] * 4,
-        out_specs=(vmem,) * 5,
+        out_specs=(vmem, vmem, hbm, hbm, hbm),
+        scratch_shapes=[
+            pltpu.VMEM((HEADS, LATENT, VHEAD), F32),
+            pltpu.VMEM((TILES, TILE // HEADS, HEADS, QUERY), F32),
+            pltpu.SemaphoreType.DMA((X + HEADS + TILES,)),
+        ],
         compiler_params=pltpu.CompilerParams(vmem_limit_bytes=16 << 20),
         name="unpack_grads",
     )(*sums)

time: 79.3 us -> 79.3 us (level)
  no operation moved by 1% of the time
where the time goes in v9:
time: 79.3 us; the launch traced here: 79.1 us
  Pallas kernels  78.5 us (99%)
    pallas_call x1, Pallas kernels, shards(): pl.pallas_call(kernel, out_shape=(jax.ShapeDtypeStruct((BLOCK, WIDTH), F3...  76.2 us
    pallas_call x1, Pallas kernels, shards(): pl.pallas_call(unpack, out_shape=(jax.ShapeDtypeStruct((2, PKEYS, WIDTH),...  2.27 us

profile of v9, /device:TPU:32, one launch (start us, length us, event | category | flops | bytes accessed | tf_op | source)
XLA Modules:
  0.0 79.1 jit_solution(15846157795040425822)
XLA Ops:
  0.6 76.2 %latent_backward.1 = (f32[32,576]{1,0:T(8,128)S(1)}, bf16[512,512]{1,0:T(8,128)(2,1)S(1)}, f32[4,512,128]{2,1,0:T(8,128)S(1)}, f32[192,640]{1,0:T(8,128)S(1)}) custom-call(bf16[2,8,576]{2,1,0:T(8,128)(2,1)} %prompt_any.1, bf16[1,16,576]{2,1,0:T(8,128)(2,1)} %suffix_any.1, bf16[160,4,192]{2,1,0:T(4,128)(2,1)} %bitcast.12, bf16[512,512]{1,0:T(8,128)(2,1)} %bitcast.10, ...), custom_call_target="tpu_custom_call" | custom-call | flops 8000000000 | bytes 6000000 | tf_op jit(solution)/shard_map/latent_backward/pallas_call | solution.py:598
  76.9 2.3 %unpack_grads.1 = (f32[2,8,576]{2,1,0:T(8,128)}, f32[1,16,576]{2,1,0:T(8,128)}, f32[160,4,192]{2,1,0:T(4,128)}, f32[512,512]{1,0:T(8,128)}, f32[2048,128]{1,0:T(8,128)}) custom-call(f32[32,576]{1,0:T(8,128)S(1)} %get-tuple-element.14.keys_ref, bf16[512,512]{1,0:T(8,128)(2,1)S(1)} %get-tuple-element.15.value_ref, ...), custom_call_target="tpu_custom_call" | custom-call | tf_op jit(solution)/shard_map/unpack_grads/pallas_call | solution.py:672

commit v10 on v9

--- a/solution.py
+++ b/solution.py
@@ -183,14 +183,13 @@
         lgr_t[:, rows] = grad.T
         return carry
 
-    for made in loads[2:]:
-        made.wait()
-    lax.fori_loop(0, 2, project, 0)
     relay(1, pl.ds(0, half))
     relay(3, pl.ds(half, half))
     spread_y(1)
     spread_y(3)
-    lax.fori_loop(2, TILES, project, 0)
+    for made in loads[2:]:
+        made.wait()
+    lax.fori_loop(0, TILES, project, 0)
 
     def gather_rows(f, carry):
         limit, prompt = carry
@@ -560,30 +559,20 @@
 def unpack(
     keys_ref, value_ref, key_up_ref, query_ref,
     prompt_out, suffix_out, query_out, key_up_out, value_up_out,
-    value_f, query_f, sem,
 ):
-    copies = []
-
-    def put(src, dst):
-        made = pltpu.make_async_copy(src, dst, sem.at[len(copies)])
-        made.start()
-        copies.append(made)
-
-    for b in range(X):
-        put(key_up_ref.at[b], key_up_out.at[:, pl.ds(b * TILE, TILE)])
-    for h in range(HEADS):
-        value_f[h] = value_ref[:, h * VHEAD : (h + 1) * VHEAD].astype(F32)
-        put(value_f.at[h], value_up_out.at[pl.ds(h * LATENT, LATENT), :])
     prompt_out[0] = keys_ref[:PKEYS, :]
     prompt_out[1] = keys_ref[PKEYS : 2 * PKEYS, :]
     suffix_out[0] = keys_ref[2 * PKEYS :, :]
+    for h in range(HEADS):
+        value_up_out[h * LATENT : (h + 1) * LATENT, :] = value_ref[
+            :, h * VHEAD : (h + 1) * VHEAD
+        ].astype(F32)
+    for b in range(X):
+        key_up_out[:, b * TILE : (b + 1) * TILE] = key_up_ref[b]
     steps = TILE // HEADS
     for t in range(TILES):
         part = query_ref[:, t * TILE : (t + 1) * TILE].T
-        query_f[t] = part.reshape(steps, HEADS, QUERY)
-        put(query_f.at[t], query_out.at[pl.ds(t * steps, steps)])
-    for made in copies:
-        made.wait()
+        query_out[t * steps : (t + 1) * steps] = part.reshape(steps, HEADS, QUERY)
 
 
 def shards(prompt, suffix, queries, key_up, value_up, out_grad, fork_prompt, suffix_length):
@@ -679,12 +668,7 @@
             jax.ShapeDtypeStruct((HEADS * LATENT, VHEAD), F32),
         ),
         in_specs=[vmem] * 4,
-        out_specs=(vmem, vmem, hbm, hbm, hbm),
-        scratch_shapes=[
-            pltpu.VMEM((HEADS, LATENT, VHEAD), F32),
-            pltpu.VMEM((TILES, TILE // HEADS, HEADS, QUERY), F32),
-            pltpu.SemaphoreType.DMA((X + HEADS + TILES,)),
-        ],
+        out_specs=(vmem,) * 5,
         compiler_params=pltpu.CompilerParams(vmem_limit_bytes=16 << 20),
         name="unpack_grads",
     )(*sums)

time: 79.3 us -> 80.7 us (1.018)
  Pallas kernels: 78.5 us -> 79.9 us
    pallas_call x1, Pallas kernels: 76.2 us -> 78 us  [shards(): pl.pallas_call(kernel, out_shape=(jax.ShapeDtypeStruct((BLOCK, WIDTH), F3...]
where the time goes in v10:
time: 80.7 us; the launch traced here: 80.5 us
  Pallas kernels  79.9 us (99%)
    pallas_call x1, Pallas kernels, shards(): pl.pallas_call(kernel, out_shape=(jax.ShapeDtypeStruct((BLOCK, WIDTH), F3...  78 us
    pallas_call x1, Pallas kernels, shards(): pl.pallas_call(unpack, out_shape=(jax.ShapeDtypeStruct((2, PKEYS, WIDTH),...  1.86 us

profile of v10, /device:TPU:32, one launch (start us, length us, event | category | flops | bytes accessed | tf_op | source)
XLA Modules:
  0.0 80.5 jit_solution(7406039262023703810)
XLA Ops:
  0.6 78.0 %latent_backward.1 = (f32[32,576]{1,0:T(8,128)S(1)}, bf16[512,512]{1,0:T(8,128)(2,1)S(1)}, f32[4,512,128]{2,1,0:T(8,128)S(1)}, f32[192,640]{1,0:T(8,128)S(1)}) custom-call(bf16[2,8,576]{2,1,0:T(8,128)(2,1)} %prompt_any.1, bf16[1,16,576]{2,1,0:T(8,128)(2,1)} %suffix_any.1, bf16[160,4,192]{2,1,0:T(4,128)(2,1)} %bitcast.12, bf16[512,512]{1,0:T(8,128)(2,1)} %bitcast.10, ...), custom_call_target="tpu_custom_call" | custom-call | flops 8000000000 | bytes 6000000 | tf_op jit(solution)/shard_map/latent_backward/pallas_call | solution.py:587
  78.7 1.9 %unpack_grads.1 = (f32[2,8,576]{2,1,0:T(8,128)}, f32[1,16,576]{2,1,0:T(8,128)}, f32[160,4,192]{2,1,0:T(4,128)}, f32[512,512]{1,0:T(8,128)}, f32[2048,128]{1,0:T(8,128)}) custom-call(f32[32,576]{1,0:T(8,128)S(1)} %get-tuple-element.14.keys_ref, bf16[512,512]{1,0:T(8,128)(2,1)S(1)} %get-tuple-element.15.value_ref, ...), custom_call_target="tpu_custom_call" | custom-call | tf_op jit(solution)/shard_map/unpack_grads/pallas_call | solution.py:661
